TPU v7x, 32 devices: a whole 2x2x4 slice. The times are simulated.
32 devices in a mesh: member: 2 (over x), lat: 16 (over z, y, core).
Axes of the slice: x: 2, y: 2, z: 4, core: 2. Of those that a mesh axis runs over, the one named last changes fastest.
Arguments:
- field: bfloat16 [512, 64, 256], P(('member', 'lat')), parts along dimension 0, may hold values from -6 to 6
- row_start: int32 [256], P('lat'), may hold values from 0 to 250, as said below
- row_count: int32 [256], P('lat'), may hold values from 6 to 13
- tap_count: int32 [256], P('lat'), may hold values from 3 to 7, as said below
- basis: bfloat16 [256, 13, 7, 9], P('lat'), may hold values from -2 to 2
- mixing: bfloat16 [2304, 256], replicated, may hold values from -0.125 to 0.125
- cotangent: bfloat16 [512, 64, 256], P(('member', 'lat')), parts along dimension 0, may hold values from -6 to 6
Outputs:
- hidden: bfloat16 [512, 64, 256], P(('member', 'lat')), parts along dimension 0
- field_grad: bfloat16 [512, 64, 256], P(('member', 'lat')), parts along dimension 0
- mixing_grad: float32 [4608, 256], P(('member', 'lat')), parts along dimension 0
There are 2 independent parts, one for each index of `member`. A program takes and returns all parts, laid end to end along the dimension named above; an argument that names none is the same for every part. Nothing has to cross between parts.
Inputs may be any that keep to these rules, and one draw needn't show every extreme that they name: Output row o reads input rows row_start[o] to row_start[o] + row_count[o] - 1; they contain o and lie within 6 rows of it. `tap_count`: Odd; wider toward the poles.
All inputs are finite; a program needn't handle non-finite values.
Results may differ from a plain program's by a relative error of at most 0.007.
Values may be sent and summed in bfloat16 or wider, within the bound.
A program may use at most 128 MiB of HBM per device.

v0:
```python
import jax
import jax.numpy as jnp
from jax import lax
from jax.sharding import PartitionSpec as P


def from_behind(block, axis, distance):
    devices = range(lax.axis_size(axis))
    route = [(i - distance, i) for i in devices if i - distance in devices]
    return lax.ppermute(block, axis, route)


def exact_gelu(values):
    return jax.nn.gelu(values, approximate=False)


def local(field, row_start, row_count, tap_count, basis, mixing, cotangent):
    rows_dev, lon_count, channels = field.shape
    slot_count, tap_total, basis_count = (basis.shape[1], basis.shape[2], basis.shape[3])
    reach = (slot_count - 1) // 2
    lane_count = lon_count * channels
    centre = tap_total // 2
    band_index = lax.axis_index("lat")
    flat_rows = field.reshape(rows_dev, lane_count)
    near_rows = [
        from_behind(piece, "lat", step)
        for step, piece in ((1, flat_rows[rows_dev - reach :]), (-1, flat_rows[:reach]))
    ]
    tail_rows = jnp.zeros((slot_count, lane_count), jnp.bfloat16)
    row_stack = jnp.concatenate([near_rows[0], flat_rows, near_rows[1], tail_rows], axis=0)
    stack_len = row_stack.shape[0]
    first_row = band_index * rows_dev - reach
    local_start = row_start - first_row
    slot_ids = jnp.arange(slot_count, dtype=jnp.int32)
    tap_ids = jnp.arange(tap_total, dtype=jnp.int32)
    slot_mask = (slot_ids[None, :] < row_count[:, None]).astype(jnp.float32)
    tap_mask = (jnp.abs(tap_ids - centre)[None, :] <= (tap_count // 2)[:, None]).astype(jnp.float32)
    masked = basis.astype(jnp.float32) * slot_mask[:, :, None, None] * tap_mask[:, None, :, None]
    weights = (
        masked.transpose(0, 2, 3, 1)
        .reshape(rows_dev, tap_total * basis_count, slot_count)
        .astype(jnp.bfloat16)
    )

    def row_forward(row_item):
        row_weights, window_start = row_item
        window = lax.dynamic_slice_in_dim(row_stack, window_start, slot_count, 0)
        partial_sum = jnp.dot(row_weights, window, preferred_element_type=jnp.float32)
        partial_sum = partial_sum.reshape(tap_total, basis_count, lon_count, channels)
        summed = sum(
            (
                jnp.roll(partial_sum[tap_index], centre - tap_index, axis=1)
                for tap_index in range(tap_total)
            )
        )
        return (
            summed.transpose(1, 0, 2)
            .reshape(lon_count, basis_count * channels)
            .astype(jnp.bfloat16)
        )

    features = lax.map(row_forward, (weights, local_start))
    feature_rows = features.reshape(rows_dev * lon_count, basis_count * channels)
    pre_act = jnp.dot(feature_rows, mixing, preferred_element_type=jnp.float32)
    activated, gelu_pull = jax.vjp(exact_gelu, pre_act)
    hidden = activated.astype(jnp.bfloat16).reshape(rows_dev, lon_count, channels)
    pre_grad = gelu_pull(cotangent.reshape(rows_dev * lon_count, channels).astype(jnp.float32))[
        0
    ].astype(jnp.bfloat16)
    feature_grad = lax.dot_general(
        pre_grad, mixing, (((1,), (1,)), ((), ())), preferred_element_type=jnp.float32
    ).astype(jnp.bfloat16)
    mixing_grad = lax.psum_scatter(
        lax.dot_general(
            feature_rows, pre_grad, (((0,), (0,)), ((), ())), preferred_element_type=jnp.float32
        ),
        "lat",
        scatter_dimension=0,
        tiled=True,
    )

    def row_contrib(row_weights, row_grad):
        grad_lanes = row_grad.reshape(lon_count, basis_count, channels).transpose(1, 0, 2)
        rolled = jnp.stack(
            [jnp.roll(grad_lanes, tap_index - centre, axis=1) for tap_index in range(tap_total)]
        )
        rolled = rolled.reshape(tap_total * basis_count, lane_count)
        return lax.dot_general(
            row_weights, rolled, (((0,), (0,)), ((), ())), preferred_element_type=jnp.float32
        )

    block_rows = 4
    window_len = block_rows + slot_count - 1
    grad_by_row = feature_grad.reshape(rows_dev, lon_count, basis_count * channels)
    window_ids = jnp.arange(window_len, dtype=jnp.int32)

    def block_back(block_number, running):
        block_first = block_number * block_rows
        block_weights = lax.dynamic_slice_in_dim(weights, block_first, block_rows, 0)
        block_grads = lax.dynamic_slice_in_dim(grad_by_row, block_first, block_rows, 0)
        block_starts = lax.dynamic_slice_in_dim(local_start, block_first, block_rows, 0)
        contribs = jax.vmap(row_contrib)(block_weights, block_grads)
        window_low = (block_first + reach - reach).astype(jnp.int32)
        targets = (block_starts[:, None] + slot_ids[None, :] - window_low).reshape(
            block_rows * slot_count
        )
        placing = (window_ids[:, None] == targets[None, :]).astype(jnp.float32)
        added = jnp.dot(
            placing,
            contribs.reshape(block_rows * slot_count, lane_count),
            precision=lax.Precision.HIGHEST,
            preferred_element_type=jnp.float32,
        )
        current = lax.dynamic_slice_in_dim(running, window_low, window_len, 0)
        return lax.dynamic_update_slice_in_dim(running, current + added, window_low, 0)

    stack_grad = lax.fori_loop(
        0, rows_dev // block_rows, block_back, jnp.zeros((stack_len, lane_count), jnp.float32)
    )
    own_rows = stack_grad[reach : reach + rows_dev]
    low_part = stack_grad[:reach]
    high_part = stack_grad[reach + rows_dev : 2 * reach + rows_dev]
    back_rows = [
        from_behind(piece.astype(jnp.bfloat16), "lat", step).astype(piece.dtype)
        for step, piece in ((-1, low_part), (1, high_part))
    ]
    filler = jnp.zeros((rows_dev - reach, lane_count), jnp.float32)
    field_sum = (
        own_rows
        + jnp.concatenate([filler, back_rows[0]], axis=0)
        + jnp.concatenate([back_rows[1], filler], axis=0)
    )
    field_grad = field_sum.astype(jnp.bfloat16).reshape(rows_dev, lon_count, channels)
    return (hidden, field_grad, mixing_grad)


def solution(mesh):
    placed = (
        P(("member", "lat"), None, None),
        P("lat"),
        P("lat"),
        P("lat"),
        P("lat", None, None, None),
        P(),
        P(("member", "lat"), None, None),
    )
    return jax.shard_map(
        local,
        mesh=mesh,
        in_specs=placed,
        out_specs=(
            P(("member", "lat"), None, None),
            P(("member", "lat"), None, None),
            P(("member", "lat"), None),
        ),
        check_vma=False,
    )
```

profile of v0, /device:TPU:16, one launch (start us, length us, event | category | flops | bytes accessed | tf_op | source)
XLA Modules:
  0.0 477.7 jit_solution(9475161790038115643)
XLA Ops:
  8.5 2.8 collective-permute-start.1
  17.2 2.8 collective-permute-done
  21.7 192.3 %while.28 = (s32[]{:T(128)}, bf16[16,64,2304]{2,1,0:T(8,128)(2,1)}, bf16[16,63,13]{1,2,0:T(8,128)(2,1)S(1)}, s32[16]{0:T(128)S(1)}, bf16[41,16384]{1,0:T(8,128)(2,1)}, /*index=5*/s32[]{:T(128)}, s32[]{:T(128)}, s32[]{:T(128)}) while((s32[]{:T(128)}, bf16[16,64,2304]{2,1,0:T(8,128)(2,1)}, bf16[16,63,13]{1,2,0:T(8,128)(2,1)S(1)}, ...), condition=%wide.region_1.2_spmd, body=%wide.region_0.1_spmd.sunk | while | flops 28753924 | bytes 48533652 | solution.py:62
  214.0 7.4 %fusion.32 = (bf16[1024,256]{1,0:T(8,128)(2,1)S(1)}, f32[1024,256]{1,0:T(8,128)}, f32[1024,256]{1,0:T(8,128)}) fusion(bf16[16,64,256]{2,1,0:T(8,128)(2,1)S(1)} %copy-done.8, bf16[1024,2304]{1,0:T(8,128)(2,1)} %bitcast.176, bf16[2304,256]{1,0:T(8,128)(2,1)S(1)} %copy-done), kind=kOutput, calls=%fused_computation.48 | convolution fusion | flops 1227096064 | bytes 9043968 | tf_op jit(solution)/shard_map/dot_general | solution.py:64
  221.3 2.9 fusion.51
  224.2 3.7 convolution_convert_fusion
  229.9 225.4 %while.29 = (s32[]{:T(128)}, f32[41,16384]{1,0:T(8,128)}, s32[16]{0:T(128)S(1)}, bf16[16,63,13]{1,2,0:T(8,128)(2,1)S(1)}, bf16[16,64,2304]{2,1,0:T(8,128)(2,1)},...) while((s32[]{:T(128)}, f32[41,16384]{1,0:T(8,128)}, s32[16]{0:T(128)S(1)}, ...), condition=%wide.region_3.4_spmd.clone, body=%wide.region_2.3_spmd.clone.sunk | while | flops 285344672 | bytes 101152616 | solution.py:117
  244.8 12.5 %copy.105 = bf16[4,7,9,64,256]{4,3,2,1,0:T(8,128)(2,1)} copy(bf16[4,7,9,64,256]{4,2,3,0,1:T(8,128)(2,1)} %bitcast.141) | data formatting | bytes 16515072 | tf_op jit(solution)/shard_map/while/body/eval_jaxpr/vmap()/transpose | solution.py:87
  257.4 9.3 %reshape.201 = bf16[4,63,16384]{2,1,0:T(8,128)(2,1)} reshape(bf16[4,7,9,64,256]{4,3,2,1,0:T(8,128)(2,1)} %copy.105) | data formatting | bytes 16515072 | tf_op jit(solution)/shard_map/while/body/eval_jaxpr/vmap()/reshape | solution.py:87
  266.7 6.6 %fusion.102 = f32[4,13,16384]{2,1,0:T(8,128)} fusion(bf16[4,63,16384]{2,1,0:T(8,128)(2,1)} %reshape.201, bf16[16,63,13]{1,2,0:T(8,128)(2,1)S(1)} %copy-done.6, s32[]{:T(128)S(6)} %select_n.45), kind=kOutput, calls=%fused_computation.30.clone.1 | convolution fusion | flops 107347968 | bytes 11681796 | tf_op jit(solution)/shard_map/while/body/eval_jaxpr/vmap()/dot_general | solution.py:88
  273.3 4.5 reshape.202
  277.8 4.0 convolution_add_fusion.2
  281.8 4.7 dynamic_update_slice.22
  301.5 12.3 %copy.105 = bf16[4,7,9,64,256]{4,3,2,1,0:T(8,128)(2,1)} copy(bf16[4,7,9,64,256]{4,2,3,0,1:T(8,128)(2,1)} %bitcast.141) | data formatting | bytes 16515072 | tf_op jit(solution)/shard_map/while/body/eval_jaxpr/vmap()/transpose | solution.py:87
  313.8 9.3 %reshape.201 = bf16[4,63,16384]{2,1,0:T(8,128)(2,1)} reshape(bf16[4,7,9,64,256]{4,3,2,1,0:T(8,128)(2,1)} %copy.105) | data formatting | bytes 16515072 | tf_op jit(solution)/shard_map/while/body/eval_jaxpr/vmap()/reshape | solution.py:87
  323.1 6.6 %fusion.102 = f32[4,13,16384]{2,1,0:T(8,128)} fusion(bf16[4,63,16384]{2,1,0:T(8,128)(2,1)} %reshape.201, bf16[16,63,13]{1,2,0:T(8,128)(2,1)S(1)} %copy-done.6, s32[]{:T(128)S(6)} %select_n.45), kind=kOutput, calls=%fused_computation.30.clone.1 | convolution fusion | flops 107347968 | bytes 11681796 | tf_op jit(solution)/shard_map/while/body/eval_jaxpr/vmap()/dot_general | solution.py:88
  329.7 4.5 reshape.202
  334.1 3.9 convolution_add_fusion.2
  338.1 4.7 dynamic_update_slice.22
  357.7 12.3 %copy.105 = bf16[4,7,9,64,256]{4,3,2,1,0:T(8,128)(2,1)} copy(bf16[4,7,9,64,256]{4,2,3,0,1:T(8,128)(2,1)} %bitcast.141) | data formatting | bytes 16515072 | tf_op jit(solution)/shard_map/while/body/eval_jaxpr/vmap()/transpose | solution.py:87
  370.1 9.3 %reshape.201 = bf16[4,63,16384]{2,1,0:T(8,128)(2,1)} reshape(bf16[4,7,9,64,256]{4,3,2,1,0:T(8,128)(2,1)} %copy.105) | data formatting | bytes 16515072 | tf_op jit(solution)/shard_map/while/body/eval_jaxpr/vmap()/reshape | solution.py:87
  379.3 6.6 %fusion.102 = f32[4,13,16384]{2,1,0:T(8,128)} fusion(bf16[4,63,16384]{2,1,0:T(8,128)(2,1)} %reshape.201, bf16[16,63,13]{1,2,0:T(8,128)(2,1)S(1)} %copy-done.6, s32[]{:T(128)S(6)} %select_n.45), kind=kOutput, calls=%fused_computation.30.clone.1 | convolution fusion | flops 107347968 | bytes 11681796 | tf_op jit(solution)/shard_map/while/body/eval_jaxpr/vmap()/dot_general | solution.py:88
  385.9 4.5 reshape.202
  390.4 3.9 convolution_add_fusion.2
  394.3 4.7 dynamic_update_slice.22
  414.0 12.3 %copy.105 = bf16[4,7,9,64,256]{4,3,2,1,0:T(8,128)(2,1)} copy(bf16[4,7,9,64,256]{4,2,3,0,1:T(8,128)(2,1)} %bitcast.141) | data formatting | bytes 16515072 | tf_op jit(solution)/shard_map/while/body/eval_jaxpr/vmap()/transpose | solution.py:87
  426.3 9.3 %reshape.201 = bf16[4,63,16384]{2,1,0:T(8,128)(2,1)} reshape(bf16[4,7,9,64,256]{4,3,2,1,0:T(8,128)(2,1)} %copy.105) | data formatting | bytes 16515072 | tf_op jit(solution)/shard_map/while/body/eval_jaxpr/vmap()/reshape | solution.py:87
  435.6 6.6 %fusion.102 = f32[4,13,16384]{2,1,0:T(8,128)} fusion(bf16[4,63,16384]{2,1,0:T(8,128)(2,1)} %reshape.201, bf16[16,63,13]{1,2,0:T(8,128)(2,1)S(1)} %copy-done.6, s32[]{:T(128)S(6)} %select_n.45), kind=kOutput, calls=%fused_computation.30.clone.1 | convolution fusion | flops 107347968 | bytes 11681796 | tf_op jit(solution)/shard_map/while/body/eval_jaxpr/vmap()/dot_general | solution.py:88
  442.2 4.5 reshape.202
  446.6 3.9 convolution_add_fusion.2
  450.5 4.7 dynamic_update_slice.22
  463.6 4.7 collective-permute-done.3
  (742 shorter events, 238.2 us)
Async XLA Ops:
  7.2 206.8 %copy-start = (bf16[2304,256]{1,0:T(8,128)(2,1)S(1)}, bf16[2304,256]{1,0:T(8,128)(2,1)}, u32[]{:S(2)}) copy-start(bf16[2304,256]{1,0:T(8,128)(2,1)} %param.16) | copy-start | bytes 3538948
  7.2 9.6 %copy-start.2 = (bf16[16,64,256]{2,1,0:T(8,128)(2,1)S(1)}, bf16[16,64,256]{2,1,0:T(8,128)(2,1)}, u32[]{:S(2)}) copy-start(bf16[16,64,256]{2,1,0:T(8,128)(2,1)} %param.11) | copy-start | bytes 1572868
  7.2 10.0 %copy-start.9 = (s32[16]{0:T(128)S(1)}, s32[16]{0:T(128)}, u32[]{:S(2)}) copy-start(s32[16]{0:T(128)} %param.12) | copy-start | bytes 196
  7.2 463.7 %reduce-scatter.2.cloned.1.call-start = ((), (), s32[]{:S(2)}) async-start(), calls=%async_computation.1 | async-start | bytes 2506752 | tf_op jit(solution)/shard_map/reduce_scatter | solution.py:73
  8.5 8.6 %collective-permute-start.1 = (bf16[6,16384]{1,0:T(8,128)(2,1)S(1)}, bf16[6,16384]{1,0:T(8,128)(2,1)S(1)}, u32[]{:S(2)}, u32[]{:S(2)}) collective-permute-start(bf16[6,16384]{1,0:T(8,128)(2,1)S(1)} %bitcast.174), channel_id=1, source_target_pairs={{1,0},{2,1},{3,2},{4,3},{5,4},{6,5},{7,6},{8,7},{9,8},{10,9},{11,1... | collective-permute-start | bytes 589832 | tf_op jit(solution)/shard_map/ppermute | solution.py:10
  11.4 8.6 %collective-permute-start = (bf16[6,16384]{1,0:T(8,128)(2,1)S(1)}, bf16[6,16384]{1,0:T(8,128)(2,1)S(1)}, u32[]{:S(2)}, u32[]{:S(2)}) collective-permute-start(bf16[6,16384]{1,0:T(8,128)(2,1)S(1)} %bitcast.175), channel_id=1, source_target_pairs={{0,1},{1,2},{2,3},{3,4},{4,5},{5,6},{6,7},{7,8},{8,9},{9,10},{10,1... | collective-permute-start | bytes 589832 | tf_op jit(solution)/shard_map/ppermute | solution.py:10
  21.7 192.3 %copy-start.8 = (bf16[16,64,256]{2,1,0:T(8,128)(2,1)S(1)}, bf16[16,64,256]{2,1,0:T(8,128)(2,1)}, u32[]{:S(2)}) copy-start(bf16[16,64,256]{2,1,0:T(8,128)(2,1)} %param.17) | copy-start | bytes 1572868
  214.0 7.4 %copy-start.7 = (bf16[16,64,2304]{2,1,0:T(8,128)(2,1)S(1)}, bf16[16,64,2304]{2,1,0:T(8,128)(2,1)}, u32[]{:S(2)}) copy-start(bf16[16,64,2304]{2,1,0:T(8,128)(2,1)} %get-tuple-element.258) | copy-start | bytes 14155780
  229.9 0.6 copy-start.5
  257.4 9.3 %copy-start.6 = (bf16[16,63,13]{1,2,0:T(8,128)(2,1)S(1)}, bf16[16,63,13]{1,2,0:T(8,128)(2,1)}, u32[]{:S(2)}) copy-start(bf16[16,63,13]{1,2,0:T(8,128)(2,1)} %copy-done.5) | copy-start | bytes 78628 | tf_op jit(solution)/shard_map/while
  286.5 0.6 copy-start.5
  313.8 9.3 %copy-start.6 = (bf16[16,63,13]{1,2,0:T(8,128)(2,1)S(1)}, bf16[16,63,13]{1,2,0:T(8,128)(2,1)}, u32[]{:S(2)}) copy-start(bf16[16,63,13]{1,2,0:T(8,128)(2,1)} %copy-done.5) | copy-start | bytes 78628 | tf_op jit(solution)/shard_map/while
  342.8 0.6 copy-start.5
  370.1 9.3 %copy-start.6 = (bf16[16,63,13]{1,2,0:T(8,128)(2,1)S(1)}, bf16[16,63,13]{1,2,0:T(8,128)(2,1)}, u32[]{:S(2)}) copy-start(bf16[16,63,13]{1,2,0:T(8,128)(2,1)} %copy-done.5) | copy-start | bytes 78628 | tf_op jit(solution)/shard_map/while
  399.0 0.6 copy-start.5
  426.3 9.3 %copy-start.6 = (bf16[16,63,13]{1,2,0:T(8,128)(2,1)S(1)}, bf16[16,63,13]{1,2,0:T(8,128)(2,1)}, u32[]{:S(2)}) copy-start(bf16[16,63,13]{1,2,0:T(8,128)(2,1)} %copy-done.5) | copy-start | bytes 78628 | tf_op jit(solution)/shard_map/while
  455.3 6.8 %copy-start.3 = (f32[1024,256]{1,0:T(8,128)S(1)}, f32[1024,256]{1,0:T(8,128)}, u32[]{:S(2)}) copy-start(f32[1024,256]{1,0:T(8,128)} %get-tuple-element.309) | copy-start | bytes 3145732
  455.3 6.8 %copy-start.4 = (f32[1024,256]{1,0:T(8,128)S(1)}, f32[1024,256]{1,0:T(8,128)}, u32[]{:S(2)}) copy-start(f32[1024,256]{1,0:T(8,128)} %get-tuple-element.333) | copy-start | bytes 3145732
  457.5 13.4 %copy-start.1 = (bf16[2304,256]{1,0:T(8,128)(2,1)S(1)}, bf16[2304,256]{1,0:T(8,128)(2,1)}, u32[]{:S(2)}) copy-start(bf16[2304,256]{1,0:T(8,128)(2,1)} %param.16) | copy-start | bytes 3538948
  457.6 6.0 %collective-permute-start.2 = (bf16[6,16384]{1,0:T(8,128)(2,1)S(1)}, bf16[6,16384]{1,0:T(8,128)(2,1)S(1)}, u32[]{:S(2)}, u32[]{:S(2)}) collective-permute-start(bf16[6,16384]{1,0:T(8,128)(2,1)S(1)} %get-tuple-element.329), channel_id=1, source_target_pairs={{1,0},{2,1},{3,2},{4,3},{5,4},{6,5},{7,6},{8,7},{9,8},{10,9},{11,1... | collective-permute-start | bytes 589832 | tf_op jit(solution)/shard_map/ppermute | solution.py:10
  459.7 8.6 %collective-permute-start.3 = (bf16[6,16384]{1,0:T(8,128)(2,1)S(1)}, bf16[6,16384]{1,0:T(8,128)(2,1)S(1)}, u32[]{:S(2)}, u32[]{:S(2)}) collective-permute-start(bf16[6,16384]{1,0:T(8,128)(2,1)S(1)} %get-tuple-element.330), channel_id=1, source_target_pairs={{0,1},{1,2},{2,3},{3,4},{4,5},{5,6},{6,7},{7,8},{8,9},{9,10},{10,1... | collective-permute-start | bytes 589832 | tf_op jit(solution)/shard_map/ppermute | solution.py:10
Sparse Core Ops, SparseCore 0:
  228.0 62.0 reduce-scatter.1
where the time goes:
time: 480 us; the launch traced here: 478 us
  local copies, waits for them, and re-layouts  260 us (54%)
  matrix products  86 us (18%)
  other arithmetic  64.3 us (13%)
  loops' own time  35.7 us (7%)
  between operations  14.2 us (3%)
  starting transfers between devices  9.17 us (2%)
  waiting for transfers between devices  8.15 us (2%)
    while x324, local copies, waits for them, and re-layouts  77.9 us
    transpose x4, local copies, waits for them, and re-layouts, row_contrib(): rolled = rolled.reshape(tap_total * basis_count, lane_count)  49.5 us
    reshape x4, local copies, waits for them, and re-layouts, row_contrib(): rolled = rolled.reshape(tap_total * basis_count, lane_count)  37.2 us
    another operation x1, loops' own time, local(): features = lax.map(row_forward, (weights, local_start))  35.4 us
    while x20, other arithmetic  32.6 us
    dot_general x16, matrix products, row_forward(): jnp.dot(row_weights, window, preferred_element_type=jnp.float32)  30 us
    dot_general x4, matrix products, row_contrib(): lax.dot_general(row_weights, rolled, (((0,), (0,)), ((), ())), preferred_...  26.4 us
    dynamic_update_slice x4, local copies, waits for them, and re-layouts, block_back(): lax.dynamic_update_slice_in_dim(running, current + added, window_low, 0)  18.9 us
  transfers between devices with their start and end apart: 5, of which 3 were waited for; matrix products, arithmetic and copies ran while one was open for 49% of the time, Pallas kernels for 0%

commit v1 on v0

v1 whole, which is shorter than its diff:
```python
import jax
import jax.numpy as jnp
from jax import lax
from jax.experimental import pallas as pl
from jax.experimental.pallas import tpu as pltpu
from jax.sharding import PartitionSpec as P

BF16 = jnp.bfloat16
F32 = jnp.float32
TILE = 16


def from_behind(block, axis, distance):
    devices = range(lax.axis_size(axis))
    route = [(i - distance, i) for i in devices if i - distance in devices]
    return lax.ppermute(block, axis, route)


def dot(a, b, dims=((1,), (0,))):
    return lax.dot_general(a, b, (dims, ((), ())), preferred_element_type=F32)


def swap_matrix():
    side = TILE * TILE
    row = lax.broadcasted_iota(jnp.int32, (side, side), 0)
    col = lax.broadcasted_iota(jnp.int32, (side, side), 1)
    return jnp.where((row & (TILE - 1)) * TILE + (row >> 4) == col, 1.0, 0.0).astype(BF16)


def fwd_kernel(dims, field, low, high, wf, mix, cot, hidden, pre_grad, mix_grad, x, feat, halo):
    lon, ch, kb, taps, reach = dims
    centre = taps // 2
    band = 2 * TILE
    blocks = lon // TILE
    side = TILE * TILE
    swap = swap_matrix()
    halo[0:reach] = low[...]
    halo[reach : 2 * reach] = high[...]
    halo[2 * reach :] = jnp.zeros((TILE - 2 * reach, lon, ch), BF16)
    for b in range(blocks):
        at = slice(b * TILE, (b + 1) * TILE)
        own_t = dot(swap, field[:, at, :].reshape(side, ch)).astype(BF16)
        halo_t = dot(swap, halo[:, at, :].reshape(side, ch)).astype(BF16)
        both = jnp.concatenate(
            [own_t.reshape(TILE, TILE, ch), halo_t.reshape(TILE, TILE, ch)], axis=1
        )
        x[(centre + b * TILE) * band : (centre + (b + 1) * TILE) * band, :] = both.reshape(
            TILE * band, ch
        )
    x[0 : centre * band, :] = x[lon * band : (lon + centre) * band, :]
    x[(lon + centre) * band :, :] = x[centre * band : 2 * centre * band, :]

    weights = wf[...]

    @pl.loop(0, lon // 4)
    def _(q):
        for u in range(4):
            n = q * 4 + u
            window = x[pl.ds(pl.multiple_of(n * band, band), taps * band), :]
            f = dot(weights, window).astype(BF16)
            for k in range(kb):
                feat[pl.ds(pl.multiple_of(n * TILE, TILE), TILE), k * ch : (k + 1) * ch] = f[
                    k * TILE : (k + 1) * TILE
                ]

    for b in range(blocks):
        at = slice(b * TILE, (b + 1) * TILE)
        rows = slice(b * side, (b + 1) * side)
        pre = dot(feat[rows, :], mix[...])
        cot_t = dot(swap, cot[:, at, :].reshape(side, ch))
        cdf = 0.5 * (1.0 + lax.erf(pre * (0.5**0.5)))
        pdf = jnp.exp(-0.5 * pre * pre) * 0.3989422804014327
        h = (pre * cdf).astype(BF16)
        hidden[:, at, :] = dot(swap, h).astype(BF16).reshape(TILE, TILE, ch)
        pre_grad[rows, :] = (cot_t * (cdf + pre * pdf)).astype(BF16)
    for k in range(kb):
        cols = slice(k * ch, (k + 1) * ch)
        mix_grad[cols, :] = dot(feat[:, cols], pre_grad[...], ((0,), (0,)))


def bwd_kernel(dims, pre_grad, mix, wb, own, low, high, grads, acc):
    lon, ch, kb, taps, reach = dims
    centre = taps // 2
    band = 2 * TILE
    blocks = lon // TILE
    side = TILE * TILE
    swap = swap_matrix()
    for k in range(kb):
        fg = dot(pre_grad[...], mix[k * ch : (k + 1) * ch, :], ((1,), (1,))).astype(BF16)
        grads[:, k * TILE : (k + 1) * TILE, :] = fg.reshape(lon, TILE, ch)
    acc[...] = jnp.zeros_like(acc)
    weights = wb[...]

    @pl.loop(0, lon // 4)
    def _(q):
        for u in range(4):
            n = q * 4 + u
            at = pl.ds(pl.multiple_of(n * band, band), taps * band)
            acc[at, :] += dot(weights, grads[n])

    acc[lon * band : (lon + centre) * band, :] += acc[0 : centre * band, :]
    acc[centre * band : 2 * centre * band, :] += acc[(lon + centre) * band :, :]
    for b in range(blocks):
        at = slice(b * TILE, (b + 1) * TILE)
        blk = acc[(centre + b * TILE) * band : (centre + (b + 1) * TILE) * band, :]
        blk = blk.reshape(TILE, band, ch)
        mine = blk[:, :TILE, :].reshape(side, ch)
        top = mine.astype(BF16)
        rest = (mine - top.astype(F32)).astype(BF16)
        own[:, at, :] = (dot(swap, top) + dot(swap, rest)).reshape(TILE, TILE, ch)
        near = dot(swap, blk[:, TILE:, :].reshape(side, ch).astype(BF16)).astype(BF16)
        near = near.reshape(TILE, TILE, ch)
        low[:, at, :] = near[:reach]
        high[:, at, :] = near[reach : 2 * reach]


def swap_with(block, step, size, ids):
    route = [(i, ids(i, step)) for i in range(size)]
    return lax.ppermute(block, "lat", route)


def sum_over_bands(partial, shard_rows, channels):
    size = lax.axis_size("lat")
    if size != 16:
        return lax.psum_scatter(partial, "lat", scatter_dimension=0, tiled=True)
    me = lax.axis_index("lat")
    core, row, depth = me & 1, (me >> 1) & 1, me >> 2
    left = partial.reshape(4, 2, 2, shard_rows, channels)

    def take(array, index, axis):
        return lax.dynamic_index_in_dim(array, index, axis, keepdims=False)

    got = swap_with(take(left, 1 - core, 2).astype(BF16), 1, size, lambda i, s: i ^ 1)
    left = take(left, core, 2) + got.astype(F32)
    got = swap_with(take(left, 1 - row, 1).astype(BF16), 1, size, lambda i, s: i ^ 2)
    left = take(left, row, 1) + got.astype(F32)
    total = take(left, depth, 0)
    for step in (1, 2, 3):
        piece = take(left, (depth + step) & 3, 0).astype(BF16)
        got = swap_with(piece, step, size, lambda i, s: (i + 4 * s) % 16)
        total = total + got.astype(F32)
    return total


def local(field, row_start, row_count, tap_count, basis, mixing, cotangent):
    rows_dev, lon, ch = field.shape
    slots, taps, kb = basis.shape[1:]
    reach = (slots - 1) // 2
    band = 2 * TILE
    dims = (lon, ch, kb, taps, reach)
    centre = taps // 2
    low_in = from_behind(field[rows_dev - reach :], "lat", 1)
    high_in = from_behind(field[:reach], "lat", -1)

    first_row = lax.axis_index("lat") * rows_dev - reach
    slot_ids = jnp.arange(slots, dtype=jnp.int32)
    tap_ids = jnp.arange(taps, dtype=jnp.int32)
    at_row = (row_start - first_row)[:, None] + slot_ids[None, :]
    place = jnp.where(
        at_row < reach,
        at_row + TILE,
        jnp.where(at_row < reach + rows_dev, at_row - reach, at_row),
    )
    placing = (place[:, :, None] == jnp.arange(band, dtype=jnp.int32)) & (
        slot_ids[None, :] < row_count[:, None]
    )[:, :, None]
    tap_mask = jnp.abs(tap_ids - centre)[None, :] <= (tap_count // 2)[:, None]
    masked = jnp.where(tap_mask[:, None, :, None], basis, jnp.zeros((), BF16))
    placed = lax.dot_general(
        masked.reshape(rows_dev, slots, taps * kb),
        placing.astype(BF16),
        (((1,), (1,)), ((0,), (0,))),
        preferred_element_type=F32,
    ).astype(BF16)
    placed = placed.reshape(rows_dev, taps, kb, band)
    wf = placed.transpose(2, 0, 1, 3).reshape(kb * rows_dev, taps * band)
    wb = wf.T

    rows = rows_dev * lon
    vmem = pl.BlockSpec(memory_space=pltpu.VMEM)
    hidden, pre_grad, mix_part = pl.pallas_call(
        lambda *refs: fwd_kernel(dims, *refs),
        out_shape=(
            jax.ShapeDtypeStruct((rows_dev, lon, ch), BF16),
            jax.ShapeDtypeStruct((rows, ch), BF16),
            jax.ShapeDtypeStruct((kb * ch, ch), F32),
        ),
        in_specs=[vmem] * 6,
        out_specs=(vmem,) * 3,
        scratch_shapes=[
            pltpu.VMEM(((lon + taps - 1) * band, ch), BF16),
            pltpu.VMEM((rows, kb * ch), BF16),
            pltpu.VMEM((TILE, lon, ch), BF16),
        ],
        compiler_params=pltpu.CompilerParams(vmem_limit_bytes=40 * 2**20),
        cost_estimate=pl.CostEstimate(
            flops=6 * rows * kb * ch * ch, bytes_accessed=8 * 2**20, transcendentals=2 * rows * ch
        ),
        name="features_hidden_mixing_grad",
    )(field, low_in, high_in, wf, mixing, cotangent)

    own, low, high = pl.pallas_call(
        lambda *refs: bwd_kernel(dims, *refs),
        out_shape=(
            jax.ShapeDtypeStruct((rows_dev, lon, ch), F32),
            jax.ShapeDtypeStruct((reach, lon, ch), BF16),
            jax.ShapeDtypeStruct((reach, lon, ch), BF16),
        ),
        in_specs=[vmem] * 3,
        out_specs=(vmem,) * 3,
        scratch_shapes=[
            pltpu.VMEM((lon, kb * TILE, ch), BF16),
            pltpu.VMEM(((lon + taps - 1) * band, ch), F32),
        ],
        compiler_params=pltpu.CompilerParams(vmem_limit_bytes=40 * 2**20),
        cost_estimate=pl.CostEstimate(
            flops=4 * rows * kb * ch * ch, bytes_accessed=8 * 2**20, transcendentals=0
        ),
        name="field_grad_of_band",
    )(pre_grad, mixing, wb)

    mixing_grad = sum_over_bands(mix_part, kb * ch // lax.axis_size("lat"), ch)
    from_high = from_behind(low, "lat", -1).astype(F32)
    from_low = from_behind(high, "lat", 1).astype(F32)
    filler = jnp.zeros((rows_dev - reach, lon, ch), F32)
    field_grad = (
        own
        + jnp.concatenate([filler, from_high], axis=0)
        + jnp.concatenate([from_low, filler], axis=0)
    ).astype(BF16)
    return (hidden, field_grad, mixing_grad)


def solution(mesh):
    placed = (
        P(("member", "lat"), None, None),
        P("lat"),
        P("lat"),
        P("lat"),
        P("lat", None, None, None),
        P(),
        P(("member", "lat"), None, None),
    )
    return jax.shard_map(
        local,
        mesh=mesh,
        in_specs=placed,
        out_specs=(
            P(("member", "lat"), None, None),
            P(("member", "lat"), None, None),
            P(("member", "lat"), None),
        ),
        check_vma=False,
    )
```

time: 480 us -> 61.6 us (0.13)
  the two profiles are of different devices: /device:TPU:16 before, /device:TPU:0 now
where the time goes in v1:
time: 61.6 us; the launch traced here: 61.2 us
  starting transfers between devices  21.1 us (34%)
  Pallas kernels  16.6 us (27%)
  local copies, waits for them, and re-layouts  10.4 us (17%)
  waiting for transfers between devices  7.22 us (12%)
  other arithmetic  4.76 us (8%)
  between operations  0.89 us (1%)
    ppermute x5, starting transfers between devices, swap_with(): return lax.ppermute(block, 'lat', route)  14.1 us
    pallas_call x1, Pallas kernels, local(): pl.pallas_call(lambda *refs: fwd_kernel(dims, *refs), out_shape=(jax.Shap...  9.72 us
    unnamed x28, local copies, waits for them, and re-layouts  7.56 us
    ppermute x5, waiting for transfers between devices, swap_with(): return lax.ppermute(block, 'lat', route)  7.2 us
    ppermute x4, starting transfers between devices, from_behind(): return lax.ppermute(block, axis, route)  6.93 us
    pallas_call x1, Pallas kernels, local(): pl.pallas_call(lambda *refs: bwd_kernel(dims, *refs), out_shape=(jax.Shap...  6.85 us
  transfers between devices with their start and end apart: 9, of which 3 were waited for; matrix products, arithmetic and copies ran while one was open for 8% of the time, Pallas kernels for 11%

profile of v1, /device:TPU:0, one launch (start us, length us, event | category | flops | bytes accessed | tf_op | source)
XLA Modules:
  0.0 61.2 jit_solution(12878614016236234724)
XLA Ops:
  0.7 1.1 %fusion.13 = (bf16[6,64,256]{2,1,0:T(8,128)(2,1)S(1)}, bf16[6,64,256]{2,1,0:T(8,128)(2,1)S(1)}) fusion(bf16[16,64,256]{2,1,0:T(8,128)(2,1)} %refs_0_.1), kind=kLoop, calls=%fused_computation.36 | loop fusion | bytes 786432 | tf_op jit(solution)/shard_map/slice | solution.py:153
  1.7 2.4 %collective-permute-start = (bf16[6,64,256]{2,1,0:T(8,128)(2,1)S(1)}, bf16[6,64,256]{2,1,0:T(8,128)(2,1)S(1)}, u32[]{:S(2)}, u32[]{:S(2)}) collective-permute-start(bf16[6,64,256]{2,1,0:T(8,128)(2,1)S(1)} %get-tuple-element.19), channel_id=1, source_target_pairs={{0,1},{1,2},{2,3},{3,4},{4,5},{5,6},{6,7},{7,8},{8,9},{9,10},{10,1... | collective-permute-start | bytes 589832 | tf_op jit(solution)/shard_map/ppermute | solution.py:16
  4.1 1.3 %collective-permute-start.1 = (bf16[6,64,256]{2,1,0:T(8,128)(2,1)S(1)}, bf16[6,64,256]{2,1,0:T(8,128)(2,1)S(1)}, u32[]{:S(2)}, u32[]{:S(2)}) collective-permute-start(bf16[6,64,256]{2,1,0:T(8,128)(2,1)S(1)} %get-tuple-element.18), channel_id=1, source_target_pairs={{1,0},{2,1},{3,2},{4,3},{5,4},{6,5},{7,6},{8,7},{9,8},{10,9},{11,1... | collective-permute-start | bytes 589832 | tf_op jit(solution)/shard_map/ppermute | solution.py:16
  5.4 0.7 %and_select_fusion = s32[16]{0:T(128)S(1)} fusion(s32[16]{0:T(128)} %param.10), kind=kLoop, calls=%fused_computation.30 | loop fusion | flops 240 | bytes 128 | tf_op jit(solution)/shard_map/jit(floor_divide)/jit(_where)/select_n | solution.py:167
  6.1 1.0 %broadcast_select_fusion = bf16[16,13,7,9]{0,2,3,1:T(8,128)(2,1)S(1)} fusion(bf16[16,13,7,9]{0,2,3,1:T(8,128)(2,1)} %param.11, pred[16,7]{0,1:T(8,128)(4,1)S(1)} %broadcast_compare_fusion), kind=kLoop, calls=%fused_computation.8 | loop fusion | flops 13104 | bytes 52528 | tf_op jit(solution)/shard_map/jit(_where)/select_n | solution.py:168
  7.1 0.7 %copy.21 = bf16[16,13,7,9]{3,2,1,0:T(8,128)(2,1)S(1)} copy(bf16[16,13,7,9]{0,2,3,1:T(8,128)(2,1)S(1)} %broadcast_select_fusion) | data formatting | bytes 52416 | tf_op jit(solution)/shard_map/reshape | solution.py:170
  7.9 0.3 reshape.106
  8.3 0.3 convolution_convert_fusion
  8.7 0.3 copy.16
  9.3 0.7 %copy-done.4 = bf16[6,64,256]{2,1,0:T(8,128)(2,1)} copy-done((bf16[6,64,256]{2,1,0:T(8,128)(2,1)}, bf16[6,64,256]{2,1,0:T(8,128)(2,1)S(1)}, u32[]{:S(2)}) %copy-start.4) | copy-done | bytes 196632
  9.9 0.7 %copy-done.6 = bf16[6,64,256]{2,1,0:T(8,128)(2,1)} copy-done((bf16[6,64,256]{2,1,0:T(8,128)(2,1)}, bf16[6,64,256]{2,1,0:T(8,128)(2,1)S(1)}, u32[]{:S(2)}) %copy-start.6) | copy-done | bytes 196632
  10.6 1.3 %copy-done.1 = bf16[2304,256]{1,0:T(8,128)(2,1)S(1)} copy-done((bf16[2304,256]{1,0:T(8,128)(2,1)S(1)}, bf16[2304,256]{1,0:T(8,128)(2,1)}, u32[]{:S(2)}) %copy-start.1) | copy-done | bytes 1179672
  11.9 0.9 %copy-done.5 = bf16[6,64,256]{2,1,0:T(8,128)(2,1)S(1)} copy-done((bf16[6,64,256]{2,1,0:T(8,128)(2,1)S(1)}, bf16[6,64,256]{2,1,0:T(8,128)(2,1)}, u32[]{:S(2)}) %copy-start.5) | copy-done | bytes 196632
  12.8 0.9 %copy-done.7 = bf16[6,64,256]{2,1,0:T(8,128)(2,1)S(1)} copy-done((bf16[6,64,256]{2,1,0:T(8,128)(2,1)S(1)}, bf16[6,64,256]{2,1,0:T(8,128)(2,1)}, u32[]{:S(2)}) %copy-start.7) | copy-done | bytes 196632
  13.7 9.7 %features_hidden_mixing_grad.1 = (bf16[16,64,256]{2,1,0:T(8,128)(2,1)}, bf16[1024,256]{1,0:T(8,128)(2,1)S(1)}, f32[2304,256]{1,0:T(8,128)S(1)}) custom-call(bf16[16,64,256]{2,1,0:T(8,128)(2,1)S(1)} %copy-done, bf16[6,64,256]{2,1,0:T(8,128)(2,1)S(1)} %copy-done.5, bf16[6,64,256]{2,1,0:T(8,128)(2,1)S(1)} %copy-done.7, bf16[144,224]{1,0:T(8,128)(2,1)S(1)} %reshape.104.refs_3_, ...), custom_call_target="tpu_custom_call" | custom-call | flops 3623878656 | bytes 8388608 | tf_op jit(solution)/shard_map/features_hidden_mixing_grad/pallas_call | solution.py:181
  23.5 0.8 %copy-done.8 = bf16[1024,256]{1,0:T(8,128)(2,1)} copy-done((bf16[1024,256]{1,0:T(8,128)(2,1)}, bf16[1024,256]{1,0:T(8,128)(2,1)S(1)}, u32[]{:S(2)}) %copy-start.8) | copy-done | bytes 524312
  24.3 3.8 %collective-permute-start.4 = (bf16[4,2,144,256]{3,2,0,1:T(8,128)(2,1)S(1)}, bf16[4,2,144,256]{3,2,0,1:T(8,128)(2,1)}, u32[]{:S(2)}, u32[]{:S(2)}) collective-permute-start(bf16[4,2,144,256]{3,2,0,1:T(8,128)(2,1)S(1)} %fusion), channel_id=1, source_target_pairs={{0,1},{1,0},{2,3},{3,2},{4,5},{5,4},{6,7},{7,6},{8,9},{9,8},{10,11... | collective-permute-start | bytes 1769480 | tf_op jit(solution)/shard_map/ppermute | solution.py:119
  28.2 1.8 %collective-permute-done.4 = bf16[4,2,144,256]{3,2,0,1:T(8,128)(2,1)} collective-permute-done((bf16[4,2,144,256]{3,2,0,1:T(8,128)(2,1)S(1)}, bf16[4,2,144,256]{3,2,0,1:T(8,128)(2,1)}, u32[]{:S(2)}, u32[]{:S(2)}) %collective-permute-start.4) | collective-permute-done | bytes 589856 | tf_op jit(solution)/shard_map/ppermute | solution.py:119
  29.9 1.2 %bitcast_add_fusion = f32[4,2,144,256]{3,2,0,1:T(8,128)S(1)} fusion(bf16[4,2,144,256]{3,2,0,1:T(8,128)(2,1)} %collective-permute-done.4, f32[4,2,2,144,256]{4,3,2,1,0:T(8,128)S(1)} %bitcast.27, s32[]{:T(128)S(6)} %select_n.55), kind=kLoop, calls=%fused_computation.1 | loop fusion | flops 589824 | bytes 2949124 | tf_op jit(solution)/shard_map/add | solution.py:134
  31.2 1.0 %copy-done.10 = f32[4,2,144,256]{3,2,0,1:T(8,128)} copy-done((f32[4,2,144,256]{3,2,0,1:T(8,128)}, f32[4,2,144,256]{3,2,0,1:T(8,128)S(1)}, u32[]{:S(2)}) %copy-start.10) | copy-done | bytes 1179672
  32.2 2.4 %collective-permute-start.5 = (bf16[4,144,256]{2,1,0:T(8,128)(2,1)S(1)}, bf16[4,144,256]{2,1,0:T(8,128)(2,1)S(1)}, u32[]{:S(2)}, u32[]{:S(2)}) collective-permute-start(bf16[4,144,256]{2,1,0:T(8,128)(2,1)S(1)} %fusion.1), channel_id=1, source_target_pairs={{0,2},{1,3},{2,0},{3,1},{4,6},{5,7},{6,4},{7,5},{8,10},{9,11},{10,... | collective-permute-start | bytes 884744 | tf_op jit(solution)/shard_map/ppermute | solution.py:119
  34.8 1.3 %copy-done.2 = bf16[2304,256]{1,0:T(8,128)(2,1)S(1)} copy-done((bf16[2304,256]{1,0:T(8,128)(2,1)S(1)}, bf16[2304,256]{1,0:T(8,128)(2,1)}, u32[]{:S(2)}) %copy-start.2) | copy-done | bytes 1179672
  36.0 6.9 %field_grad_of_band.1 = (f32[16,64,256]{2,1,0:T(8,128)S(1)}, bf16[6,64,256]{2,1,0:T(8,128)(2,1)S(1)}, bf16[6,64,256]{2,1,0:T(8,128)(2,1)S(1)}) custom-call(bf16[1024,256]{1,0:T(8,128)(2,1)S(1)} %copy-done.9, bf16[2304,256]{1,0:T(8,128)(2,1)S(1)} %copy-done.2, bf16[224,144]{1,0:T(8,128)(2,1)S(1)} %bitcast.28), custom_call_target="tpu_custom_call" | custom-call | flops 2415919104 | bytes 8388608 | tf_op jit(solution)/shard_map/field_grad_of_band/pallas_call | solution.py:202
  42.9 2.0 %collective-permute-start.3 = (bf16[6,64,256]{2,1,0:T(8,128)(2,1)S(1)}, bf16[6,64,256]{2,1,0:T(8,128)(2,1)S(1)}, u32[]{:S(2)}, u32[]{:S(2)}) collective-permute-start(bf16[6,64,256]{2,1,0:T(8,128)(2,1)S(1)} %get-tuple-element.13), channel_id=1, source_target_pairs={{0,1},{1,2},{2,3},{3,4},{4,5},{5,6},{6,7},{7,8},{8,9},{9,10},{10,1... | collective-permute-start | bytes 589832 | tf_op jit(solution)/shard_map/ppermute | solution.py:16
  44.9 1.3 %collective-permute-start.2 = (bf16[6,64,256]{2,1,0:T(8,128)(2,1)S(1)}, bf16[6,64,256]{2,1,0:T(8,128)(2,1)S(1)}, u32[]{:S(2)}, u32[]{:S(2)}) collective-permute-start(bf16[6,64,256]{2,1,0:T(8,128)(2,1)S(1)} %get-tuple-element.12), channel_id=1, source_target_pairs={{1,0},{2,1},{3,2},{4,3},{5,4},{6,5},{7,6},{8,7},{9,8},{10,9},{11,1... | collective-permute-start | bytes 589832 | tf_op jit(solution)/shard_map/ppermute | solution.py:16
  46.3 5.9 %collective-permute-start.8 = (bf16[144,256]{1,0:T(8,128)(2,1)S(1)}, bf16[144,256]{1,0:T(8,128)(2,1)S(1)}, u32[]{:S(2)}, u32[]{:S(2)}) collective-permute-start(bf16[144,256]{1,0:T(8,128)(2,1)S(1)} %get-tuple-element.16), channel_id=1, source_target_pairs={{0,12},{1,13},{2,14},{3,15},{4,0},{5,1},{6,2},{7,3},{8,4},{9,5},{1... | collective-permute-start | bytes 221192 | tf_op jit(solution)/shard_map/ppermute | solution.py:119
  52.2 0.4 collective-permute-start.7
  52.6 1.6 %collective-permute-start.6 = (bf16[144,256]{1,0:T(8,128)(2,1)S(1)}, bf16[144,256]{1,0:T(8,128)(2,1)S(1)}, u32[]{:S(2)}, u32[]{:S(2)}) collective-permute-start(bf16[144,256]{1,0:T(8,128)(2,1)S(1)} %get-tuple-element.15), channel_id=1, source_target_pairs={{0,4},{1,5},{2,6},{3,7},{4,8},{5,9},{6,10},{7,11},{8,12},{9,13},{1... | collective-permute-start | bytes 221192 | tf_op jit(solution)/shard_map/ppermute | solution.py:119
  54.2 0.9 %add_convert_fusion = bf16[16,64,256]{2,1,0:T(8,128)(2,1)} fusion(f32[16,64,256]{2,1,0:T(8,128)S(1)} %get-tuple-element.11, bf16[6,64,256]{2,1,0:T(8,128)(2,1)S(1)} %collective-permute-done.3, bf16[6,64,256]{2,1,0:T(8,128)(2,1)S(1)} %collective-permute-done.2), kind=kLoop, calls=%fused_computation.3 | loop fusion | flops 1310720 | bytes 1966080 | tf_op jit(solution)/shard_map/convert_element_type | solution.py:230
  55.1 1.9 %collective-permute-done.8 = bf16[144,256]{1,0:T(8,128)(2,1)S(1)} collective-permute-done((bf16[144,256]{1,0:T(8,128)(2,1)S(1)}, bf16[144,256]{1,0:T(8,128)(2,1)S(1)}, u32[]{:S(2)}, u32[]{:S(2)}) %collective-permute-start.8) | collective-permute-done | bytes 73760 | tf_op jit(solution)/shard_map/ppermute | solution.py:119
  56.9 3.6 %collective-permute-done.7 = bf16[144,256]{1,0:T(8,128)(2,1)S(1)} collective-permute-done((bf16[144,256]{1,0:T(8,128)(2,1)S(1)}, bf16[144,256]{1,0:T(8,128)(2,1)S(1)}, u32[]{:S(2)}, u32[]{:S(2)}) %collective-permute-start.7) | collective-permute-done | bytes 73760 | tf_op jit(solution)/shard_map/ppermute | solution.py:119
  60.5 0.7 %fusion.3 = f32[144,256]{1,0:T(8,128)} fusion(bf16[144,256]{1,0:T(8,128)(2,1)S(1)} %collective-permute-done.8, bf16[144,256]{1,0:T(8,128)(2,1)S(1)} %collective-permute-done.7, bf16[144,256]{1,0:T(8,128)(2,1)S(1)} %collective-permute-done.6, f32[4,144,256]{2,1,0:T(8,128)S(1)} %bitcast_add_fusion.1, s32[]{:T(128)S(6)} %select_n.59), kind=kLoop, calls=%fused_computation.11 | loop fusion | flops 221184 | bytes 516100 | tf_op jit(solution)/shard_map/add | solution.py:141
  (38 shorter events, 0.9 us)
Async XLA Ops:
  0.6 7.5 %copy-start.13 = (s32[16]{0:T(128)S(1)}, s32[16]{0:T(128)}, u32[]{:S(2)}) copy-start(s32[16]{0:T(128)} %param.8) | copy-start | bytes 196
  0.6 7.6 %copy-start.12 = (s32[16]{0:T(128)S(1)}, s32[16]{0:T(128)}, u32[]{:S(2)}) copy-start(s32[16]{0:T(128)} %param.9) | copy-start | bytes 196
  1.7 7.5 %collective-permute-start = (bf16[6,64,256]{2,1,0:T(8,128)(2,1)S(1)}, bf16[6,64,256]{2,1,0:T(8,128)(2,1)S(1)}, u32[]{:S(2)}, u32[]{:S(2)}) collective-permute-start(bf16[6,64,256]{2,1,0:T(8,128)(2,1)S(1)} %get-tuple-element.19), channel_id=1, source_target_pairs={{0,1},{1,2},{2,3},{3,4},{4,5},{5,6},{6,7},{7,8},{8,9},{9,10},{10,1... | collective-permute-start | bytes 589832 | tf_op jit(solution)/shard_map/ppermute | solution.py:16
  4.1 5.8 %collective-permute-start.1 = (bf16[6,64,256]{2,1,0:T(8,128)(2,1)S(1)}, bf16[6,64,256]{2,1,0:T(8,128)(2,1)S(1)}, u32[]{:S(2)}, u32[]{:S(2)}) collective-permute-start(bf16[6,64,256]{2,1,0:T(8,128)(2,1)S(1)} %get-tuple-element.18), channel_id=1, source_target_pairs={{1,0},{2,1},{3,2},{4,3},{5,4},{6,5},{7,6},{8,7},{9,8},{10,9},{11,1... | collective-permute-start | bytes 589832 | tf_op jit(solution)/shard_map/ppermute | solution.py:16
  7.9 2.8 %copy-start = (bf16[16,64,256]{2,1,0:T(8,128)(2,1)S(1)}, bf16[16,64,256]{2,1,0:T(8,128)(2,1)}, u32[]{:S(2)}) copy-start(bf16[16,64,256]{2,1,0:T(8,128)(2,1)} %refs_0_.1) | copy-start | bytes 1572868
  7.9 2.7 %copy-start.3 = (bf16[16,64,256]{2,1,0:T(8,128)(2,1)S(1)}, bf16[16,64,256]{2,1,0:T(8,128)(2,1)}, u32[]{:S(2)}) copy-start(bf16[16,64,256]{2,1,0:T(8,128)(2,1)} %refs_5_.1) | copy-start | bytes 1572868
  9.2 0.7 %copy-start.4 = (bf16[6,64,256]{2,1,0:T(8,128)(2,1)}, bf16[6,64,256]{2,1,0:T(8,128)(2,1)S(1)}, u32[]{:S(2)}) copy-start(bf16[6,64,256]{2,1,0:T(8,128)(2,1)S(1)} %collective-permute-done.refs_1_) | copy-start | bytes 589828
  9.9 0.7 %copy-start.6 = (bf16[6,64,256]{2,1,0:T(8,128)(2,1)}, bf16[6,64,256]{2,1,0:T(8,128)(2,1)S(1)}, u32[]{:S(2)}) copy-start(bf16[6,64,256]{2,1,0:T(8,128)(2,1)S(1)} %collective-permute-done.1.refs_2_) | copy-start | bytes 589828
  10.6 1.3 %copy-start.1 = (bf16[2304,256]{1,0:T(8,128)(2,1)S(1)}, bf16[2304,256]{1,0:T(8,128)(2,1)}, u32[]{:S(2)}) copy-start(bf16[2304,256]{1,0:T(8,128)(2,1)} %refs_1_.1) | copy-start | bytes 3538948
  11.9 0.9 %copy-start.5 = (bf16[6,64,256]{2,1,0:T(8,128)(2,1)S(1)}, bf16[6,64,256]{2,1,0:T(8,128)(2,1)}, u32[]{:S(2)}) copy-start(bf16[6,64,256]{2,1,0:T(8,128)(2,1)} %copy-done.4) | copy-start | bytes 589828
  12.8 0.9 %copy-start.7 = (bf16[6,64,256]{2,1,0:T(8,128)(2,1)S(1)}, bf16[6,64,256]{2,1,0:T(8,128)(2,1)}, u32[]{:S(2)}) copy-start(bf16[6,64,256]{2,1,0:T(8,128)(2,1)} %copy-done.6) | copy-start | bytes 589828
  23.5 0.8 %copy-start.8 = (bf16[1024,256]{1,0:T(8,128)(2,1)}, bf16[1024,256]{1,0:T(8,128)(2,1)S(1)}, u32[]{:S(2)}) copy-start(bf16[1024,256]{1,0:T(8,128)(2,1)S(1)} %get-tuple-element.10.refs_0_) | copy-start | bytes 1572868
  24.3 5.6 %collective-permute-start.4 = (bf16[4,2,144,256]{3,2,0,1:T(8,128)(2,1)S(1)}, bf16[4,2,144,256]{3,2,0,1:T(8,128)(2,1)}, u32[]{:S(2)}, u32[]{:S(2)}) collective-permute-start(bf16[4,2,144,256]{3,2,0,1:T(8,128)(2,1)S(1)} %fusion), channel_id=1, source_target_pairs={{0,1},{1,0},{2,3},{3,2},{4,5},{5,4},{6,7},{7,6},{8,9},{9,8},{10,11... | collective-permute-start | bytes 1769480 | tf_op jit(solution)/shard_map/ppermute | solution.py:119
  28.2 6.6 %copy-start.9 = (bf16[1024,256]{1,0:T(8,128)(2,1)S(1)}, bf16[1024,256]{1,0:T(8,128)(2,1)}, u32[]{:S(2)}) copy-start(bf16[1024,256]{1,0:T(8,128)(2,1)} %copy-done.8) | copy-start | bytes 1572868
  31.1 1.1 %copy-start.10 = (f32[4,2,144,256]{3,2,0,1:T(8,128)}, f32[4,2,144,256]{3,2,0,1:T(8,128)S(1)}, u32[]{:S(2)}) copy-start(f32[4,2,144,256]{3,2,0,1:T(8,128)S(1)} %bitcast_add_fusion) | copy-start | bytes 3538948
  32.2 14.0 %collective-permute-start.5 = (bf16[4,144,256]{2,1,0:T(8,128)(2,1)S(1)}, bf16[4,144,256]{2,1,0:T(8,128)(2,1)S(1)}, u32[]{:S(2)}, u32[]{:S(2)}) collective-permute-start(bf16[4,144,256]{2,1,0:T(8,128)(2,1)S(1)} %fusion.1), channel_id=1, source_target_pairs={{0,2},{1,3},{2,0},{3,1},{4,6},{5,7},{6,4},{7,5},{8,10},{9,11},{10,... | collective-permute-start | bytes 884744 | tf_op jit(solution)/shard_map/ppermute | solution.py:119
  34.7 1.3 %copy-start.2 = (bf16[2304,256]{1,0:T(8,128)(2,1)S(1)}, bf16[2304,256]{1,0:T(8,128)(2,1)}, u32[]{:S(2)}) copy-start(bf16[2304,256]{1,0:T(8,128)(2,1)} %refs_1_.1) | copy-start | bytes 3538948
  36.0 10.2 %copy-start.11 = (f32[4,2,144,256]{3,2,0,1:T(8,128)S(1)}, f32[4,2,144,256]{3,2,0,1:T(8,128)}, u32[]{:S(2)}) copy-start(f32[4,2,144,256]{3,2,0,1:T(8,128)} %copy-done.10) | copy-start | bytes 3538948
  42.9 11.3 %collective-permute-start.3 = (bf16[6,64,256]{2,1,0:T(8,128)(2,1)S(1)}, bf16[6,64,256]{2,1,0:T(8,128)(2,1)S(1)}, u32[]{:S(2)}, u32[]{:S(2)}) collective-permute-start(bf16[6,64,256]{2,1,0:T(8,128)(2,1)S(1)} %get-tuple-element.13), channel_id=1, source_target_pairs={{0,1},{1,2},{2,3},{3,4},{4,5},{5,6},{6,7},{7,8},{8,9},{9,10},{10,1... | collective-permute-start | bytes 589832 | tf_op jit(solution)/shard_map/ppermute | solution.py:16
  44.9 9.3 %collective-permute-start.2 = (bf16[6,64,256]{2,1,0:T(8,128)(2,1)S(1)}, bf16[6,64,256]{2,1,0:T(8,128)(2,1)S(1)}, u32[]{:S(2)}, u32[]{:S(2)}) collective-permute-start(bf16[6,64,256]{2,1,0:T(8,128)(2,1)S(1)} %get-tuple-element.12), channel_id=1, source_target_pairs={{1,0},{2,1},{3,2},{4,3},{5,4},{6,5},{7,6},{8,7},{9,8},{10,9},{11,1... | collective-permute-start | bytes 589832 | tf_op jit(solution)/shard_map/ppermute | solution.py:16
  46.3 10.6 %collective-permute-start.8 = (bf16[144,256]{1,0:T(8,128)(2,1)S(1)}, bf16[144,256]{1,0:T(8,128)(2,1)S(1)}, u32[]{:S(2)}, u32[]{:S(2)}) collective-permute-start(bf16[144,256]{1,0:T(8,128)(2,1)S(1)} %get-tuple-element.16), channel_id=1, source_target_pairs={{0,12},{1,13},{2,14},{3,15},{4,0},{5,1},{6,2},{7,3},{8,4},{9,5},{1... | collective-permute-start | bytes 221192 | tf_op jit(solution)/shard_map/ppermute | solution.py:119
  52.2 8.4 %collective-permute-start.7 = (bf16[144,256]{1,0:T(8,128)(2,1)S(1)}, bf16[144,256]{1,0:T(8,128)(2,1)S(1)}, u32[]{:S(2)}, u32[]{:S(2)}) collective-permute-start(bf16[144,256]{1,0:T(8,128)(2,1)S(1)} %get-tuple-element.17), channel_id=1, source_target_pairs={{0,8},{1,9},{2,10},{3,11},{4,12},{5,13},{6,14},{7,15},{8,0},{9,1},... | collective-permute-start | bytes 221192 | tf_op jit(solution)/shard_map/ppermute | solution.py:119
  52.6 7.9 %collective-permute-start.6 = (bf16[144,256]{1,0:T(8,128)(2,1)S(1)}, bf16[144,256]{1,0:T(8,128)(2,1)S(1)}, u32[]{:S(2)}, u32[]{:S(2)}) collective-permute-start(bf16[144,256]{1,0:T(8,128)(2,1)S(1)} %get-tuple-element.15), channel_id=1, source_target_pairs={{0,4},{1,5},{2,6},{3,7},{4,8},{5,9},{6,10},{7,11},{8,12},{9,13},{1... | collective-permute-start | bytes 221192 | tf_op jit(solution)/shard_map/ppermute | solution.py:119

commit v2 on v1

--- a/solution.py
+++ b/solution.py
@@ -114,32 +114,346 @@
         high[:, at, :] = near[reach : 2 * reach]
 
 
-def swap_with(block, step, size, ids):
-    route = [(i, ids(i, step)) for i in range(size)]
-    return lax.ppermute(block, "lat", route)
-
-
-def sum_over_bands(partial, shard_rows, channels):
-    size = lax.axis_size("lat")
-    if size != 16:
-        return lax.psum_scatter(partial, "lat", scatter_dimension=0, tiled=True)
+def remote(src, dst, send, recv, target):
+    return pltpu.make_async_remote_copy(
+        src_ref=src,
+        dst_ref=dst,
+        send_sem=send,
+        recv_sem=recv,
+        device_id={"lat": target},
+        device_id_type=pl.DeviceIdType.MESH,
+    )
+
+
+def fused_kernel(
+    dims, field_in, wf, wb, mix_in, cot_in, hidden, field_grad, mix_shard,
+    field, mix, cot, halo, x, feat, pre_grad, mix_grad, grads, acc, own,
+    near, got, c_out, c_in, y_out, y_in, z_out, z_in, kept,
+    l_sem, f_send, f_recv, b_send, b_recv, c_send, c_recv, y_send, y_recv, z_send, z_recv,
+):
+    lon, ch, kb, taps, reach = dims
+    centre = taps // 2
+    band = 2 * TILE
+    blocks = lon // TILE
+    side = TILE * TILE
+    rows_dev = field.shape[0]
+    shard = mix_shard.shape[0]
     me = lax.axis_index("lat")
-    core, row, depth = me & 1, (me >> 1) & 1, me >> 2
-    left = partial.reshape(4, 2, 2, shard_rows, channels)
-
-    def take(array, index, axis):
-        return lax.dynamic_index_in_dim(array, index, axis, keepdims=False)
-
-    got = swap_with(take(left, 1 - core, 2).astype(BF16), 1, size, lambda i, s: i ^ 1)
-    left = take(left, core, 2) + got.astype(F32)
-    got = swap_with(take(left, 1 - row, 1).astype(BF16), 1, size, lambda i, s: i ^ 2)
-    left = take(left, row, 1) + got.astype(F32)
-    total = take(left, depth, 0)
+    last = lax.axis_size("lat") - 1
+    core = me % 2
+    row = (me // 2) % 2
+    depth = me // 4
+    other_core = me + 1 - 2 * core
+    other_row = me + 2 - 4 * row
+    far = me - 1 + 2 * core
+    has_far = (far >= 0) & (far <= last)
+    has_low = me > 0
+    has_high = me < last
+
+    loads = [
+        pltpu.make_async_copy(src, dst, l_sem.at[i])
+        for i, (src, dst) in enumerate(((field_in, field), (cot_in, cot), (mix_in, mix)))
+    ]
+    for load in loads:
+        load.start()
+
+    barrier = pltpu.get_barrier_semaphore()
+
+    def greet(device):
+        pl.semaphore_signal(
+            barrier, inc=1, device_id={"lat": device}, device_id_type=pl.DeviceIdType.MESH
+        )
+
+    greet(other_core)
+    greet(other_row)
     for step in (1, 2, 3):
-        piece = take(left, (depth + step) & 3, 0).astype(BF16)
-        got = swap_with(piece, step, size, lambda i, s: (i + 4 * s) % 16)
-        total = total + got.astype(F32)
-    return total
+        greet((me + 4 * step) % 16)
+
+    @pl.when(has_far)
+    def _():
+        greet(far)
+
+    pl.semaphore_wait(barrier, 5 + has_far.astype(jnp.int32))
+
+    up = remote(
+        field_in.at[rows_dev - reach : rows_dev], halo.at[0:reach], f_send.at[0], f_recv.at[0],
+        me + 1,
+    )
+    down = remote(
+        field_in.at[0:reach], halo.at[reach : 2 * reach], f_send.at[1], f_recv.at[1],
+        me - 1,
+    )
+
+    @pl.when(has_high)
+    def _():
+        up.start()
+
+    @pl.when(has_low)
+    def _():
+        down.start()
+
+    none = jnp.zeros((reach, lon, ch), BF16)
+
+    @pl.when(me == 0)
+    def _():
+        halo[0:reach] = none
+        got[0:reach] = none
+
+    @pl.when(me == last)
+    def _():
+        halo[reach : 2 * reach] = none
+        got[reach : 2 * reach] = none
+
+    halo[2 * reach :] = jnp.zeros((TILE - 2 * reach, lon, ch), BF16)
+    swap = swap_matrix()
+    loads[0].wait()
+    for b in range(blocks):
+        at = slice(b * TILE, (b + 1) * TILE)
+        to = slice(centre + b * TILE, centre + (b + 1) * TILE)
+        part = dot(swap, field[:, at, :].reshape(side, ch)).astype(BF16)
+        x[to, 0:TILE, :] = part.reshape(TILE, TILE, ch)
+    loads[1].wait()
+    loads[2].wait()
+
+    @pl.when(has_low)
+    def _():
+        up.wait_recv()
+
+    @pl.when(has_high)
+    def _():
+        down.wait_recv()
+
+    for b in range(blocks):
+        at = slice(b * TILE, (b + 1) * TILE)
+        to = slice(centre + b * TILE, centre + (b + 1) * TILE)
+        part = dot(swap, halo[:, at, :].reshape(side, ch)).astype(BF16)
+        x[to, TILE:band, :] = part.reshape(TILE, TILE, ch)
+    x[0:centre] = x[lon : lon + centre]
+    x[lon + centre :] = x[centre : 2 * centre]
+
+    weights = wf[...]
+
+    @pl.loop(0, lon // 4)
+    def _(q):
+        for u in range(4):
+            n = q * 4 + u
+            window = x[pl.ds(n, taps)].reshape(taps * band, ch)
+            f = dot(weights, window).astype(BF16)
+            for k in range(kb):
+                feat[pl.ds(pl.multiple_of(n * TILE, TILE), TILE), k * ch : (k + 1) * ch] = f[
+                    k * TILE : (k + 1) * TILE
+                ]
+
+    for b in range(blocks):
+        at = slice(b * TILE, (b + 1) * TILE)
+        rows = slice(b * side, (b + 1) * side)
+        pre = dot(feat[rows, :], mix[...])
+        cot_t = dot(swap, cot[:, at, :].reshape(side, ch))
+        cdf = 0.5 * (1.0 + lax.erf(pre * (0.5**0.5)))
+        pdf = jnp.exp(-0.5 * pre * pre) * 0.3989422804014327
+        h = (pre * cdf).astype(BF16)
+        hidden[:, at, :] = dot(swap, h).astype(BF16).reshape(TILE, TILE, ch)
+        pre_grad[rows, :] = (cot_t * (cdf + pre * pdf)).astype(BF16)
+
+    def term(z, y, c):
+        first = pl.multiple_of((4 * z + 2 * y + c) * shard, TILE)
+        return mix_grad[pl.ds(first, shard), :]
+
+    def by_core(z):
+        return remote(c_out.at[z], c_in.at[z], c_send.at[z], c_recv.at[z], other_core)
+
+    def by_row(z):
+        return remote(y_out.at[z], y_in.at[z], y_send.at[z], y_recv.at[z], other_row)
+
+    def by_depth(z):
+        slot = (depth + 7 - z) % 4
+        return remote(
+            z_out.at[z], z_in.at[slot], z_send.at[z], z_recv.at[slot], 4 * z + me % 4
+        )
+
+    def send_core(z):
+        for y in range(2):
+            c_out[z, y] = term(z, y, 1 - core).astype(BF16)
+        by_core(z).start()
+
+    def send_row(z):
+        by_core(z).wait_recv()
+        y_out[z] = (term(z, 1 - row, core) + c_in[z, 1 - row].astype(F32)).astype(BF16)
+        by_row(z).start()
+
+    def send_depth(z):
+        by_row(z).wait_recv()
+        total = term(z, row, core) + c_in[z, row].astype(F32) + y_in[z].astype(F32)
+
+        @pl.when(depth == z)
+        def _():
+            kept[...] = total
+
+        @pl.when(depth != z)
+        def _():
+            z_out[z] = total.astype(BF16)
+            by_depth(z).start()
+
+    for k in range(kb):
+        cols = slice(k * ch, (k + 1) * ch)
+        mix_grad[cols, :] = dot(feat[:, cols], pre_grad[...], ((0,), (0,)))
+        done = (k + 1) * ch // (4 * shard) - 1
+        before = k * ch // (4 * shard) - 1
+        if done > before:
+            send_core(done)
+            if done > 0:
+                send_row(done - 1)
+
+    for k in range(kb):
+        fg = dot(pre_grad[...], mix[k * ch : (k + 1) * ch, :], ((1,), (1,))).astype(BF16)
+        grads[:, k * TILE : (k + 1) * TILE, :] = fg.reshape(lon, TILE, ch)
+        if k == 1:
+            send_row(3)
+        if k == 3:
+            send_depth(0)
+        if k == 6:
+            send_depth(1)
+    acc[...] = jnp.zeros_like(acc)
+    back = wb[...]
+
+    def spread(q):
+        for u in range(4):
+            n = q * 4 + u
+            at = pl.ds(pl.multiple_of(n * band, band), taps * band)
+            acc[at, :] += dot(back, grads[n])
+
+    pl.loop(0, lon // 8)(spread)
+    send_depth(2)
+    pl.loop(lon // 8, lon // 4)(spread)
+    send_depth(3)
+
+    acc[lon * band : (lon + centre) * band, :] += acc[0 : centre * band, :]
+    acc[centre * band : 2 * centre * band, :] += acc[(lon + centre) * band :, :]
+
+    def block_of(b):
+        blk = acc[(centre + b * TILE) * band : (centre + (b + 1) * TILE) * band, :]
+        return blk.reshape(TILE, band, ch)
+
+    for b in range(blocks):
+        part = block_of(b)[:, TILE:, :].reshape(side, ch).astype(BF16)
+        near[:, b * TILE : (b + 1) * TILE, :] = dot(swap, part).astype(BF16).reshape(TILE, TILE, ch)
+    to_low = remote(
+        near.at[0:reach], got.at[reach : 2 * reach], b_send.at[0], b_recv.at[0],
+        me - 1,
+    )
+    to_high = remote(
+        near.at[reach : 2 * reach], got.at[0:reach], b_send.at[1], b_recv.at[1],
+        me + 1,
+    )
+
+    @pl.when(has_low)
+    def _():
+        to_low.start()
+
+    @pl.when(has_high)
+    def _():
+        to_high.start()
+
+    for b in range(blocks):
+        mine = block_of(b)[:, :TILE, :].reshape(side, ch)
+        top = mine.astype(BF16)
+        rest = (mine - top.astype(F32)).astype(BF16)
+        own[:, b * TILE : (b + 1) * TILE, :] = (dot(swap, top) + dot(swap, rest)).reshape(
+            TILE, TILE, ch
+        )
+    field_grad[reach : rows_dev - reach] = own[reach : rows_dev - reach].astype(BF16)
+
+    @pl.when(has_high)
+    def _():
+        to_low.wait_recv()
+
+    field_grad[rows_dev - reach :] = (
+        own[rows_dev - reach :] + got[reach : 2 * reach].astype(F32)
+    ).astype(BF16)
+
+    @pl.when(has_low)
+    def _():
+        to_high.wait_recv()
+
+    field_grad[0:reach] = (own[0:reach] + got[0:reach].astype(F32)).astype(BF16)
+
+    total = kept[...]
+    for slot in range(3):
+        remote(
+            z_out.at[0], z_in.at[slot], z_send.at[0], z_recv.at[slot], other_row
+        ).wait_recv()
+        total = total + z_in[slot].astype(F32)
+    mix_shard[...] = total
+
+    @pl.when(has_high)
+    def _():
+        up.wait_send()
+        to_high.wait_send()
+
+    @pl.when(has_low)
+    def _():
+        down.wait_send()
+        to_low.wait_send()
+
+    for z in range(4):
+        by_core(z).wait_send()
+        by_row(z).wait_send()
+
+        @pl.when(depth != z)
+        def _():
+            by_depth(z).wait_send()
+
+
+def fused(dims, field, wf, wb, mixing, cotangent):
+    lon, ch, kb, taps, reach = dims
+    rows_dev = field.shape[0]
+    rows = rows_dev * lon
+    shard = kb * ch // 16
+    vmem = pl.BlockSpec(memory_space=pltpu.VMEM)
+    hbm = pl.BlockSpec(memory_space=pl.ANY)
+    band = 2 * TILE
+    sems = pltpu.SemaphoreType.DMA
+    return pl.pallas_call(
+        lambda *refs: fused_kernel(dims, *refs),
+        out_shape=(
+            jax.ShapeDtypeStruct((rows_dev, lon, ch), BF16),
+            jax.ShapeDtypeStruct((rows_dev, lon, ch), BF16),
+            jax.ShapeDtypeStruct((shard, ch), F32),
+        ),
+        in_specs=[hbm, vmem, vmem, hbm, hbm],
+        out_specs=(vmem,) * 3,
+        scratch_shapes=[
+            pltpu.VMEM((rows_dev, lon, ch), BF16),
+            pltpu.VMEM((kb * ch, ch), BF16),
+            pltpu.VMEM((rows_dev, lon, ch), BF16),
+            pltpu.VMEM((TILE, lon, ch), BF16),
+            pltpu.VMEM((lon + taps - 1, band, ch), BF16),
+            pltpu.VMEM((rows, kb * ch), BF16),
+            pltpu.VMEM((rows, ch), BF16),
+            pltpu.VMEM((kb * ch, ch), F32),
+            pltpu.VMEM((lon, kb * TILE, ch), BF16),
+            pltpu.VMEM(((lon + taps - 1) * band, ch), F32),
+            pltpu.VMEM((rows_dev, lon, ch), F32),
+            pltpu.VMEM((TILE, lon, ch), BF16),
+            pltpu.VMEM((2 * reach, lon, ch), BF16),
+            pltpu.VMEM((4, 2, shard, ch), BF16),
+            pltpu.VMEM((4, 2, shard, ch), BF16),
+            pltpu.VMEM((4, shard, ch), BF16),
+            pltpu.VMEM((4, shard, ch), BF16),
+            pltpu.VMEM((4, shard, ch), BF16),
+            pltpu.VMEM((3, shard, ch), BF16),
+            pltpu.VMEM((shard, ch), F32),
+            sems((3,)), sems((2,)), sems((2,)), sems((2,)), sems((2,)), sems((4,)),
+            sems((4,)), sems((4,)), sems((4,)), sems((4,)), sems((3,)),
+        ],
+        compiler_params=pltpu.CompilerParams(
+            vmem_limit_bytes=48 * 2**20, collective_id=0, has_side_effects=True
+        ),
+        cost_estimate=pl.CostEstimate(
+            flops=10 * rows * kb * ch * ch, bytes_accessed=8 * 2**20, transcendentals=2 * rows * ch
+        ),
+        name="conv_and_gradients",
+    )(field, wf, wb, mixing, cotangent)
 
 
 def local(field, row_start, row_count, tap_count, basis, mixing, cotangent):
@@ -149,8 +463,6 @@
     band = 2 * TILE
     dims = (lon, ch, kb, taps, reach)
     centre = taps // 2
-    low_in = from_behind(field[rows_dev - reach :], "lat", 1)
-    high_in = from_behind(field[:reach], "lat", -1)
 
     first_row = lax.axis_index("lat") * rows_dev - reach
     slot_ids = jnp.arange(slots, dtype=jnp.int32)
@@ -176,6 +488,11 @@
     wf = placed.transpose(2, 0, 1, 3).reshape(kb * rows_dev, taps * band)
     wb = wf.T
 
+    if lax.axis_size("lat") == 16:
+        return fused(dims, field, wf, wb, mixing, cotangent)
+
+    low_in = from_behind(field[rows_dev - reach :], "lat", 1)
+    high_in = from_behind(field[:reach], "lat", -1)
     rows = rows_dev * lon
     vmem = pl.BlockSpec(memory_space=pltpu.VMEM)
     hidden, pre_grad, mix_part = pl.pallas_call(
@@ -219,7 +536,7 @@
         name="field_grad_of_band",
     )(pre_grad, mixing, wb)
 
-    mixing_grad = sum_over_bands(mix_part, kb * ch // lax.axis_size("lat"), ch)
+    mixing_grad = lax.psum_scatter(mix_part, "lat", scatter_dimension=0, tiled=True)
     from_high = from_behind(low, "lat", -1).astype(F32)
     from_low = from_behind(high, "lat", 1).astype(F32)
     filler = jnp.zeros((rows_dev - reach, lon, ch), F32)

time: 61.6 us -> 45 us (0.73)
  the two profiles are of different devices: /device:TPU:0 before, /device:TPU:16 now
where the time goes in v2:
time: 45 us; the launch traced here: 44.8 us
  Pallas kernels  36.4 us (81%)
  local copies, waits for them, and re-layouts  4.12 us (9%)
  other arithmetic  3.2 us (7%)
  between operations  0.72 us (2%)
    pallas_call x1, Pallas kernels, fused(): pl.pallas_call(lambda *refs: fused_kernel(dims, *refs), out_shape=(jax.Sh...  36.4 us
    unnamed x9, local copies, waits for them, and re-layouts  2.49 us
    select_n x1, other arithmetic, local(): masked = jnp.where(tap_mask[:, None, :, None], basis, jnp.zeros((), BF16))  0.99 us
    reshape x2, local copies, waits for them, and re-layouts, local(): masked.reshape(rows_dev, slots, taps * kb)  0.98 us

profile of v2, /device:TPU:16, one launch (start us, length us, event | category | flops | bytes accessed | tf_op | source)
XLA Modules:
  0.0 44.8 jit_solution(9792430972413487203)
XLA Ops:
  0.6 0.7 %broadcast_subtract_fusion = s32[16]{0:T(128)S(1)} fusion(s32[16]{0:T(128)} %param.8, s32[]{:T(128)S(6)} %sub.21), kind=kLoop, calls=%fused_computation.17 | loop fusion | flops 16 | bytes 132 | tf_op jit(solution)/shard_map/sub | solution.py:470
  1.3 0.7 %and_select_fusion = s32[16]{0:T(128)S(1)} fusion(s32[16]{0:T(128)} %param.10), kind=kLoop, calls=%fused_computation.12 | loop fusion | flops 240 | bytes 128 | tf_op jit(solution)/shard_map/jit(floor_divide)/jit(_where)/select_n | solution.py:479
  2.0 0.1 broadcast_compare_fusion
  2.0 0.7 %iota_compare_fusion.1 = pred[16,13]{1,0:T(8,128)(4,1)S(1)} fusion(s32[16]{0:T(128)} %param.9), kind=kLoop, calls=%fused_computation.8 | loop fusion | flops 208 | bytes 272 | tf_op jit(solution)/shard_map/lt | solution.py:477
  2.8 0.1 fusion.4
  2.8 1.0 %broadcast_select_fusion = bf16[16,13,7,9]{0,2,3,1:T(8,128)(2,1)S(1)} fusion(bf16[16,13,7,9]{0,2,3,1:T(8,128)(2,1)} %param.11, pred[16,7]{0,1:T(8,128)(4,1)S(1)} %broadcast_compare_fusion), kind=kLoop, calls=%fused_computation.1 | loop fusion | flops 13104 | bytes 52528 | tf_op jit(solution)/shard_map/jit(_where)/select_n | solution.py:480
  3.8 0.7 %copy.17 = bf16[16,13,7,9]{3,2,1,0:T(8,128)(2,1)S(1)} copy(bf16[16,13,7,9]{0,2,3,1:T(8,128)(2,1)S(1)} %broadcast_select_fusion) | data formatting | bytes 52416 | tf_op jit(solution)/shard_map/reshape | solution.py:482
  4.6 0.0 copy-start
  4.6 0.0 copy-start.1
  4.6 0.0 copy-start.2
  4.6 0.3 reshape.97
  4.9 0.3 convolution_convert_fusion
  5.2 0.3 copy.14
  5.5 0.1 copy.15
  5.6 0.2 reshape.96.refs_1_
  5.8 0.1 copy.16
  5.9 0.0 copy-done
  5.9 0.1 copy-done.1
  6.0 0.2 copy-done.2
  6.1 36.4 %conv_and_gradients.1 = (bf16[16,64,256]{2,1,0:T(8,128)(2,1)S(1)}, bf16[16,64,256]{2,1,0:T(8,128)(2,1)S(1)}, f32[144,256]{1,0:T(8,128)S(1)}) custom-call(bf16[16,64,256]{2,1,0:T(8,128)(2,1)S(1)} %copy-done.1, bf16[144,224]{1,0:T(8,128)(2,1)S(1)} %reshape.96.refs_1_, bf16[224,144]{1,0:T(8,128)(2,1)S(1)} %bitcast.5, bf16[2304,256]{1,0:T(8,128)(2,1)S(1)} %copy-done, ...), custom_call_target="tpu_custom_call" | custom-call | flops 6039797760 | bytes 8388608 | tf_op jit(solution)/shard_map/conv_and_gradients/pallas_call | solution.py:416
  42.5 0.8 %copy.22 = bf16[16,64,256]{2,1,0:T(8,128)(2,1)} copy(bf16[16,64,256]{2,1,0:T(8,128)(2,1)S(1)} %get-tuple-element.6) | data formatting | bytes 1048576
  43.3 0.8 %copy.23 = bf16[16,64,256]{2,1,0:T(8,128)(2,1)} copy(bf16[16,64,256]{2,1,0:T(8,128)(2,1)S(1)} %get-tuple-element.7) | data formatting | bytes 1048576
  44.1 0.7 %copy.24 = f32[144,256]{1,0:T(8,128)} copy(f32[144,256]{1,0:T(8,128)S(1)} %get-tuple-element.8) | data formatting | bytes 294912
  (1 shorter events, 0.0 us)
Async XLA Ops:
  4.6 1.3 %copy-start = (bf16[2304,256]{1,0:T(8,128)(2,1)S(1)}, bf16[2304,256]{1,0:T(8,128)(2,1)}, u32[]{:S(2)}) copy-start(bf16[2304,256]{1,0:T(8,128)(2,1)} %refs_3_.1) | copy-start | bytes 3538948
  4.6 1.4 %copy-start.1 = (bf16[16,64,256]{2,1,0:T(8,128)(2,1)S(1)}, bf16[16,64,256]{2,1,0:T(8,128)(2,1)}, u32[]{:S(2)}) copy-start(bf16[16,64,256]{2,1,0:T(8,128)(2,1)} %refs_0_.1) | copy-start | bytes 1572868
  4.6 1.5 %copy-start.2 = (bf16[16,64,256]{2,1,0:T(8,128)(2,1)S(1)}, bf16[16,64,256]{2,1,0:T(8,128)(2,1)}, u32[]{:S(2)}) copy-start(bf16[16,64,256]{2,1,0:T(8,128)(2,1)} %refs_4_.1) | copy-start | bytes 1572868

commit v3 on v2

--- a/solution.py
+++ b/solution.py
@@ -114,6 +114,40 @@
         high[:, at, :] = near[reach : 2 * reach]
 
 
+def filter_matrix(dims, basis, start, count, tap_count, first_row):
+    lon, ch, kb, taps, reach = dims
+    slots = basis.shape[0]
+    band = 2 * TILE
+    lanes = taps * band
+    out_row = lax.broadcasted_iota(jnp.int32, (TILE, lanes), 0)
+    lane = lax.broadcasted_iota(jnp.int32, (TILE, lanes), 1)
+    place = lane & (band - 1)
+    tap = lane >> 5
+    in_row = jnp.where(
+        place < TILE, place + reach, jnp.where(place < TILE + reach, place - TILE, place)
+    )
+    first = jnp.zeros((TILE, lanes), jnp.int32)
+    used = first
+    half = first
+    for o in range(TILE):
+        here = out_row == o
+        first = jnp.where(here, start[o] - first_row, first)
+        used = jnp.where(here, count[o], used)
+        half = jnp.where(here, tap_count[o] >> 1, half)
+    slot = in_row - first
+    inside = (slot < used) & (jnp.abs(tap - taps // 2) <= half) & (place < TILE + 2 * reach)
+    slot = jnp.where(inside, slot, -1)
+    slot = jnp.concatenate([slot] * kb, axis=0)
+    to_lane = lax.broadcasted_iota(jnp.int32, (taps, lanes), 1) >> 5
+    spread = jnp.where(
+        lax.broadcasted_iota(jnp.int32, (taps, lanes), 0) == to_lane, 1.0, 0.0
+    ).astype(BF16)
+    total = jnp.zeros((kb * TILE, lanes), F32)
+    for j in range(slots):
+        total = jnp.where(slot == j, dot(basis[j], spread), total)
+    return total.astype(BF16)
+
+
 def remote(src, dst, send, recv, target):
     return pltpu.make_async_remote_copy(
         src_ref=src,
@@ -126,8 +160,8 @@
 
 
 def fused_kernel(
-    dims, field_in, wf, wb, mix_in, cot_in, hidden, field_grad, mix_shard,
-    field, mix, cot, halo, x, feat, pre_grad, mix_grad, grads, acc, own,
+    dims, field_in, basis, start, count, tap_count, mix_in, cot_in, hidden, field_grad, mix_shard,
+    wf, wb, field, mix, cot, halo, x, feat, pre_grad, mix_grad, grads, acc, own,
     near, got, c_out, c_in, y_out, y_in, z_out, z_in, kept,
     l_sem, f_send, f_recv, b_send, b_recv, c_send, c_recv, y_send, y_recv, z_send, z_recv,
 ):
@@ -212,6 +246,15 @@
         to = slice(centre + b * TILE, centre + (b + 1) * TILE)
         part = dot(swap, field[:, at, :].reshape(side, ch)).astype(BF16)
         x[to, 0:TILE, :] = part.reshape(TILE, TILE, ch)
+    wf[...] = filter_matrix(dims, basis, start, count, tap_count, me * rows_dev - reach)
+    side_k = kb * TILE
+    eye = jnp.where(
+        lax.broadcasted_iota(jnp.int32, (side_k, side_k), 0)
+        == lax.broadcasted_iota(jnp.int32, (side_k, side_k), 1),
+        1.0,
+        0.0,
+    ).astype(BF16)
+    wb[...] = dot(wf[...], eye, ((0,), (0,))).astype(BF16)
     loads[1].wait()
     loads[2].wait()
 
@@ -301,18 +344,18 @@
         before = k * ch // (4 * shard) - 1
         if done > before:
             send_core(done)
-            if done > 0:
-                send_row(done - 1)
+            if done > 1:
+                send_row(done - 2)
 
     for k in range(kb):
         fg = dot(pre_grad[...], mix[k * ch : (k + 1) * ch, :], ((1,), (1,))).astype(BF16)
         grads[:, k * TILE : (k + 1) * TILE, :] = fg.reshape(lon, TILE, ch)
         if k == 1:
+            send_row(2)
+        if k == 4:
             send_row(3)
-        if k == 3:
+        if k == 7:
             send_depth(0)
-        if k == 6:
-            send_depth(1)
     acc[...] = jnp.zeros_like(acc)
     back = wb[...]
 
@@ -322,10 +365,11 @@
             at = pl.ds(pl.multiple_of(n * band, band), taps * band)
             acc[at, :] += dot(back, grads[n])
 
-    pl.loop(0, lon // 8)(spread)
+    pl.loop(0, lon // 16)(spread)
+    send_depth(1)
+    pl.loop(lon // 16, 3 * lon // 16)(spread)
     send_depth(2)
-    pl.loop(lon // 8, lon // 4)(spread)
-    send_depth(3)
+    pl.loop(3 * lon // 16, lon // 4)(spread)
 
     acc[lon * band : (lon + centre) * band, :] += acc[0 : centre * band, :]
     acc[centre * band : 2 * centre * band, :] += acc[(lon + centre) * band :, :]
@@ -354,6 +398,7 @@
     def _():
         to_high.start()
 
+    send_depth(3)
     for b in range(blocks):
         mine = block_of(b)[:, :TILE, :].reshape(side, ch)
         top = mine.astype(BF16)
@@ -404,13 +449,14 @@
             by_depth(z).wait_send()
 
 
-def fused(dims, field, wf, wb, mixing, cotangent):
+def fused(dims, field, basis, start, count, tap_count, mixing, cotangent):
     lon, ch, kb, taps, reach = dims
     rows_dev = field.shape[0]
     rows = rows_dev * lon
     shard = kb * ch // 16
     vmem = pl.BlockSpec(memory_space=pltpu.VMEM)
     hbm = pl.BlockSpec(memory_space=pl.ANY)
+    smem = pl.BlockSpec(memory_space=pltpu.SMEM)
     band = 2 * TILE
     sems = pltpu.SemaphoreType.DMA
     return pl.pallas_call(
@@ -420,9 +466,11 @@
             jax.ShapeDtypeStruct((rows_dev, lon, ch), BF16),
             jax.ShapeDtypeStruct((shard, ch), F32),
         ),
-        in_specs=[hbm, vmem, vmem, hbm, hbm],
+        in_specs=[hbm, vmem, smem, smem, smem, hbm, hbm],
         out_specs=(vmem,) * 3,
         scratch_shapes=[
+            pltpu.VMEM((kb * TILE, taps * band), BF16),
+            pltpu.VMEM((taps * band, kb * TILE), BF16),
             pltpu.VMEM((rows_dev, lon, ch), BF16),
             pltpu.VMEM((kb * ch, ch), BF16),
             pltpu.VMEM((rows_dev, lon, ch), BF16),
@@ -453,7 +501,15 @@
             flops=10 * rows * kb * ch * ch, bytes_accessed=8 * 2**20, transcendentals=2 * rows * ch
         ),
         name="conv_and_gradients",
-    )(field, wf, wb, mixing, cotangent)
+    )(
+        field,
+        basis.transpose(1, 3, 0, 2).reshape(basis.shape[1], kb * rows_dev, taps),
+        start,
+        count,
+        tap_count,
+        mixing,
+        cotangent,
+    )
 
 
 def local(field, row_start, row_count, tap_count, basis, mixing, cotangent):
@@ -463,6 +519,8 @@
     band = 2 * TILE
     dims = (lon, ch, kb, taps, reach)
     centre = taps // 2
+    if lax.axis_size("lat") == 16:
+        return fused(dims, field, basis, row_start, row_count, tap_count, mixing, cotangent)
 
     first_row = lax.axis_index("lat") * rows_dev - reach
     slot_ids = jnp.arange(slots, dtype=jnp.int32)
@@ -488,9 +546,6 @@
     wf = placed.transpose(2, 0, 1, 3).reshape(kb * rows_dev, taps * band)
     wb = wf.T
 
-    if lax.axis_size("lat") == 16:
-        return fused(dims, field, wf, wb, mixing, cotangent)
-
     low_in = from_behind(field[rows_dev - reach :], "lat", 1)
     high_in = from_behind(field[:reach], "lat", -1)
     rows = rows_dev * lon

time: 45 us -> 46.5 us (1.033)
  local copies, waits for them, and re-layouts: 4.12 us -> 9.28 us
  other arithmetic: 3.2 us -> 0 us
    unnamed x9 -> x15, local copies, waits for them, and re-layouts: 2.49 us -> 7.56 us
    select_n x3 -> x0, other arithmetic: 1.73 us -> none  [the longest x1 0.99 us: local(): masked = jnp.where(tap_mask[:, None, :, None], basis, jnp.zeros((), BF16))]
    transpose x1, local copies, waits for them, and re-layouts: 0.08 us -> 1.72 us  [fused(): basis.transpose(1, 3, 0, 2).reshape(basis.shape[1], kb * rows_dev, taps)]
    reshape x4 -> x0, local copies, waits for them, and re-layouts: 1.27 us -> none  [the longest x2 0.98 us: local(): masked.reshape(rows_dev, slots, taps * kb)]
    lt x1 -> x0, other arithmetic: 0.73 us -> none  [local(): slot_ids[None, :] < row_count[:, None]]
    sub x1 -> x0, other arithmetic: 0.66 us -> none  [local(): at_row = (row_start - first_row)[:, None] + slot_ids[None, :]]
where the time goes in v3:
time: 46.5 us; the launch traced here: 46.1 us
  Pallas kernels  36.2 us (78%)
  local copies, waits for them, and re-layouts  9.28 us (20%)
  between operations  0.65 us (1%)
    pallas_call x1, Pallas kernels, fused(): pl.pallas_call(lambda *refs: fused_kernel(dims, *refs), out_shape=(jax.Sh...  36.2 us
    unnamed x15, local copies, waits for them, and re-layouts  7.56 us
    transpose x1, local copies, waits for them, and re-layouts, fused(): basis.transpose(1, 3, 0, 2).reshape(basis.shape[1], kb * rows_dev, taps)  1.72 us

profile of v3, /device:TPU:16, one launch (start us, length us, event | category | flops | bytes accessed | tf_op | source)
XLA Modules:
  0.0 46.1 jit_solution(18426333836497325021)
XLA Ops:
  0.6 1.7 %copy.10 = bf16[13,9,16,7]{3,2,1,0:T(8,128)(2,1)S(1)} copy(bf16[13,9,16,7]{2,3,1,0:T(8,128)(2,1)} %bitcast.3) | data formatting | bytes 52416 | tf_op jit(solution)/shard_map/transpose | solution.py:506
  2.3 0.0 copy-start
  2.4 1.3 %copy-done = bf16[2304,256]{1,0:T(8,128)(2,1)S(1)} copy-done((bf16[2304,256]{1,0:T(8,128)(2,1)S(1)}, bf16[2304,256]{1,0:T(8,128)(2,1)}, u32[]{:S(2)}) %copy-start) | copy-done | bytes 1179672
  3.6 0.0 copy-start.1
  3.6 1.0 %copy-done.1 = bf16[16,64,256]{2,1,0:T(8,128)(2,1)S(1)} copy-done((bf16[16,64,256]{2,1,0:T(8,128)(2,1)S(1)}, bf16[16,64,256]{2,1,0:T(8,128)(2,1)}, u32[]{:S(2)}) %copy-start.1) | copy-done | bytes 524312
  4.7 0.0 copy-start.2
  4.7 1.0 %copy-done.2 = bf16[16,64,256]{2,1,0:T(8,128)(2,1)S(1)} copy-done((bf16[16,64,256]{2,1,0:T(8,128)(2,1)S(1)}, bf16[16,64,256]{2,1,0:T(8,128)(2,1)}, u32[]{:S(2)}) %copy-start.2) | copy-done | bytes 524312
  5.7 0.0 copy-start.3
  5.7 0.7 %copy-done.3 = s32[16]{0:T(128)S(1)} copy-done((s32[16]{0:T(128)S(1)}, s32[16]{0:T(128)}, u32[]{:S(2)}) %copy-start.3) | copy-done | bytes 88
  6.4 0.0 copy-start.4
  6.4 0.7 %copy-done.4 = s32[16]{0:T(128)S(1)} copy-done((s32[16]{0:T(128)S(1)}, s32[16]{0:T(128)}, u32[]{:S(2)}) %copy-start.4) | copy-done | bytes 88
  7.0 0.0 copy-start.5
  7.0 0.7 %copy-done.5 = s32[16]{0:T(128)S(1)} copy-done((s32[16]{0:T(128)S(1)}, s32[16]{0:T(128)}, u32[]{:S(2)}) %copy-start.5) | copy-done | bytes 88
  7.7 36.2 %conv_and_gradients.1 = (bf16[16,64,256]{2,1,0:T(8,128)(2,1)S(1)}, bf16[16,64,256]{2,1,0:T(8,128)(2,1)S(1)}, f32[144,256]{1,0:T(8,128)S(1)}) custom-call(bf16[16,64,256]{2,1,0:T(8,128)(2,1)S(1)} %copy-done.1, bf16[13,144,7]{2,1,0:T(8,128)(2,1)S(1)} %bitcast.2, s32[16]{0:T(128)S(1)} %copy-done.3, s32[16]{0:T(128)S(1)} %copy-done.4, s32[16]{0:T(128)S(1)} %copy-done.5, ...), custom_call_target="tpu_custom_call" | custom-call | flops 6039797760 | bytes 8388608 | tf_op jit(solution)/shard_map/conv_and_gradients/pallas_call | solution.py:462
  43.9 0.8 %copy.14 = bf16[16,64,256]{2,1,0:T(8,128)(2,1)} copy(bf16[16,64,256]{2,1,0:T(8,128)(2,1)S(1)} %get-tuple-element.6) | data formatting | bytes 1048576
  44.7 0.8 %copy.15 = bf16[16,64,256]{2,1,0:T(8,128)(2,1)} copy(bf16[16,64,256]{2,1,0:T(8,128)(2,1)S(1)} %get-tuple-element.7) | data formatting | bytes 1048576
  45.5 0.7 %copy.16 = f32[144,256]{1,0:T(8,128)} copy(f32[144,256]{1,0:T(8,128)S(1)} %get-tuple-element.8) | data formatting | bytes 294912
Async XLA Ops:
  2.3 1.3 %copy-start = (bf16[2304,256]{1,0:T(8,128)(2,1)S(1)}, bf16[2304,256]{1,0:T(8,128)(2,1)}, u32[]{:S(2)}) copy-start(bf16[2304,256]{1,0:T(8,128)(2,1)} %refs_5_.1) | copy-start | bytes 3538948
  3.6 1.0 %copy-start.1 = (bf16[16,64,256]{2,1,0:T(8,128)(2,1)S(1)}, bf16[16,64,256]{2,1,0:T(8,128)(2,1)}, u32[]{:S(2)}) copy-start(bf16[16,64,256]{2,1,0:T(8,128)(2,1)} %refs_0_.1) | copy-start | bytes 1572868
  4.7 1.0 %copy-start.2 = (bf16[16,64,256]{2,1,0:T(8,128)(2,1)S(1)}, bf16[16,64,256]{2,1,0:T(8,128)(2,1)}, u32[]{:S(2)}) copy-start(bf16[16,64,256]{2,1,0:T(8,128)(2,1)} %refs_6_.1) | copy-start | bytes 1572868
  5.7 0.7 %copy-start.3 = (s32[16]{0:T(128)S(1)}, s32[16]{0:T(128)}, u32[]{:S(2)}) copy-start(s32[16]{0:T(128)} %refs_2_.1) | copy-start | bytes 196
  6.4 0.7 %copy-start.4 = (s32[16]{0:T(128)S(1)}, s32[16]{0:T(128)}, u32[]{:S(2)}) copy-start(s32[16]{0:T(128)} %refs_3_.1) | copy-start | bytes 196
  7.0 0.7 %copy-start.5 = (s32[16]{0:T(128)S(1)}, s32[16]{0:T(128)}, u32[]{:S(2)}) copy-start(s32[16]{0:T(128)} %refs_4_.1) | copy-start | bytes 196

commit v4 on v3

--- a/solution.py
+++ b/solution.py
@@ -160,8 +160,8 @@
 
 
 def fused_kernel(
-    dims, field_in, basis, start, count, tap_count, mix_in, cot_in, hidden, field_grad, mix_shard,
-    wf, wb, field, mix, cot, halo, x, feat, pre_grad, mix_grad, grads, acc, own,
+    dims, field_in, basis, start_in, count_in, taps_in, mix_in, cot_in, hidden, field_grad, mix_shard,
+    start, count, tap_count, wf, wb, field, mix, cot, halo, x, feat, pre_grad, mix_grad, grads, acc, own,
     near, got, c_out, c_in, y_out, y_in, z_out, z_in, kept,
     l_sem, f_send, f_recv, b_send, b_recv, c_send, c_recv, y_send, y_recv, z_send, z_recv,
 ):
@@ -186,7 +186,16 @@
 
     loads = [
         pltpu.make_async_copy(src, dst, l_sem.at[i])
-        for i, (src, dst) in enumerate(((field_in, field), (cot_in, cot), (mix_in, mix)))
+        for i, (src, dst) in enumerate(
+            (
+                (field_in, field),
+                (cot_in, cot),
+                (mix_in, mix),
+                (start_in, start),
+                (count_in, count),
+                (taps_in, tap_count),
+            )
+        )
     ]
     for load in loads:
         load.start()
@@ -246,6 +255,8 @@
         to = slice(centre + b * TILE, centre + (b + 1) * TILE)
         part = dot(swap, field[:, at, :].reshape(side, ch)).astype(BF16)
         x[to, 0:TILE, :] = part.reshape(TILE, TILE, ch)
+    for load in loads[3:]:
+        load.wait()
     wf[...] = filter_matrix(dims, basis, start, count, tap_count, me * rows_dev - reach)
     side_k = kb * TILE
     eye = jnp.where(
@@ -456,7 +467,6 @@
     shard = kb * ch // 16
     vmem = pl.BlockSpec(memory_space=pltpu.VMEM)
     hbm = pl.BlockSpec(memory_space=pl.ANY)
-    smem = pl.BlockSpec(memory_space=pltpu.SMEM)
     band = 2 * TILE
     sems = pltpu.SemaphoreType.DMA
     return pl.pallas_call(
@@ -466,9 +476,12 @@
             jax.ShapeDtypeStruct((rows_dev, lon, ch), BF16),
             jax.ShapeDtypeStruct((shard, ch), F32),
         ),
-        in_specs=[hbm, vmem, smem, smem, smem, hbm, hbm],
+        in_specs=[hbm, vmem, hbm, hbm, hbm, hbm, hbm],
         out_specs=(vmem,) * 3,
         scratch_shapes=[
+            pltpu.SMEM((rows_dev,), jnp.int32),
+            pltpu.SMEM((rows_dev,), jnp.int32),
+            pltpu.SMEM((rows_dev,), jnp.int32),
             pltpu.VMEM((kb * TILE, taps * band), BF16),
             pltpu.VMEM((taps * band, kb * TILE), BF16),
             pltpu.VMEM((rows_dev, lon, ch), BF16),
@@ -491,11 +504,11 @@
             pltpu.VMEM((4, shard, ch), BF16),
             pltpu.VMEM((3, shard, ch), BF16),
             pltpu.VMEM((shard, ch), F32),
-            sems((3,)), sems((2,)), sems((2,)), sems((2,)), sems((2,)), sems((4,)),
+            sems((6,)), sems((2,)), sems((2,)), sems((2,)), sems((2,)), sems((4,)),
             sems((4,)), sems((4,)), sems((4,)), sems((4,)), sems((3,)),
         ],
         compiler_params=pltpu.CompilerParams(
-            vmem_limit_bytes=48 * 2**20, collective_id=0, has_side_effects=True
+            vmem_limit_bytes=62 * 2**20, collective_id=0, has_side_effects=True
         ),
         cost_estimate=pl.CostEstimate(
             flops=10 * rows * kb * ch * ch, bytes_accessed=8 * 2**20, transcendentals=2 * rows * ch

time: 46.5 us -> 44.3 us (0.953)
  local copies, waits for them, and re-layouts: 9.28 us -> 5.88 us
  Pallas kernels: 36.2 us -> 37.5 us
    unnamed x15 -> x7, local copies, waits for them, and re-layouts: 7.56 us -> 3.41 us
    pallas_call x1, Pallas kernels: 36.2 us -> 37.5 us  [fused(): pl.pallas_call(lambda *refs: fused_kernel(dims, *refs), out_shape=(jax.Sh...]
    transpose x1, local copies, waits for them, and re-layouts: 1.72 us -> 2.47 us  [fused(): basis.transpose(1, 3, 0, 2).reshape(basis.shape[1], kb * rows_dev, taps)]
where the time goes in v4:
time: 44.3 us; the launch traced here: 44.1 us
  Pallas kernels  37.5 us (85%)
  local copies, waits for them, and re-layouts  5.88 us (13%)
  between operations  0.66 us (1%)
    pallas_call x1, Pallas kernels, fused(): pl.pallas_call(lambda *refs: fused_kernel(dims, *refs), out_shape=(jax.Sh...  37.5 us
    unnamed x7, local copies, waits for them, and re-layouts  3.41 us
    transpose x1, local copies, waits for them, and re-layouts, fused(): basis.transpose(1, 3, 0, 2).reshape(basis.shape[1], kb * rows_dev, taps)  2.47 us

profile of v4, /device:TPU:16, one launch (start us, length us, event | category | flops | bytes accessed | tf_op | source)
XLA Modules:
  0.0 44.1 jit_solution(2524419343622075672)
XLA Ops:
  0.6 2.5 %copy.10 = bf16[13,9,16,7]{3,2,1,0:T(8,128)(2,1)} copy(bf16[13,9,16,7]{2,3,1,0:T(8,128)(2,1)} %bitcast.3) | data formatting | bytes 52416 | tf_op jit(solution)/shard_map/transpose | solution.py:519
  3.1 37.5 %conv_and_gradients.1 = (bf16[16,64,256]{2,1,0:T(8,128)(2,1)}, bf16[16,64,256]{2,1,0:T(8,128)(2,1)}, f32[144,256]{1,0:T(8,128)}) custom-call(bf16[16,64,256]{2,1,0:T(8,128)(2,1)} %refs_0_.1, bf16[13,144,7]{2,1,0:T(8,128)(2,1)} %bitcast.2, s32[16]{0:T(128)} %refs_2_.1, s32[16]{0:T(128)} %refs_3_.1, s32[16]{0:T(128)} %refs_4_.1, bf16[2304,256]{1,0:T(8,128)(2,1)} %refs_5_.1, ...), custom_call_target="tpu_custom_call" | custom-call | flops 6039797760 | bytes 8388608 | tf_op jit(solution)/shard_map/conv_and_gradients/pallas_call | solution.py:472
  40.7 0.0 copy-start
  40.7 0.0 copy-start.1
  40.7 1.9 %copy.14 = bf16[16,64,256]{2,1,0:T(8,128)(2,1)} copy(bf16[16,64,256]{2,1,0:T(8,128)(2,1)} %get-tuple-element.6) | data formatting | bytes 1048576
  42.6 0.0 copy-done
  42.6 0.8 %copy.15 = bf16[16,64,256]{2,1,0:T(8,128)(2,1)} copy(bf16[16,64,256]{2,1,0:T(8,128)(2,1)S(1)} %copy-done) | data formatting | bytes 1048576
  43.4 0.0 copy-done.1
  43.4 0.7 %copy.16 = f32[144,256]{1,0:T(8,128)} copy(f32[144,256]{1,0:T(8,128)S(1)} %copy-done.1) | data formatting | bytes 294912
Async XLA Ops:
  40.7 2.0 %copy-start = (bf16[16,64,256]{2,1,0:T(8,128)(2,1)S(1)}, bf16[16,64,256]{2,1,0:T(8,128)(2,1)}, u32[]{:S(2)}) copy-start(bf16[16,64,256]{2,1,0:T(8,128)(2,1)} %get-tuple-element.7) | copy-start | bytes 1572868
  40.7 2.8 %copy-start.1 = (f32[144,256]{1,0:T(8,128)S(1)}, f32[144,256]{1,0:T(8,128)}, u32[]{:S(2)}) copy-start(f32[144,256]{1,0:T(8,128)} %get-tuple-element.8) | copy-start | bytes 442372
